TPU v7x, 256 devices: a whole 4x4x8 slice. The times are simulated.
256 devices in a mesh: row: 16 (over x_lo, y, core), col: 16 (over z, x_hi).
Axes of the slice: x: 4 (x_hi: 2, x_lo: 2; x = x_hi * 2 + x_lo), y: 4, z: 8, core: 2. Of those that a mesh axis runs over, the one named last changes fastest.
Arguments:
- candidates: bfloat16 [16384, 768], P(('row', 'col')), may hold values from -6 to 6
- targets: bfloat16 [32768, 768], P(('col', 'row')), may hold values from -6 to 6
- target_domain: int32 [32768], P(('col', 'row')), may hold values from 0 to 63
- domain_counts: int32 [64], replicated, may hold values from 1 to 999
Outputs:
- projection: bfloat16 [16384, 768], P(('row', 'col'))
- cand_potential: float32 [16384], P('row')
- tgt_potential: float32 [32768], P('col')
All inputs are finite; a program needn't handle non-finite values.
Results may differ from a plain program's by a relative error of at most 0.023.
Values may be sent and summed in bfloat16 or wider, within the bound.
No kernel may reach another device: no remote copies, remote signals or barrier semaphores. Data moves between devices by JAX's collectives and lax.ppermute only.
A program may use at most 64 MiB of HBM per device.

v0:
```python
import jax
import jax.numpy as jnp
from jax import lax
from jax.sharding import PartitionSpec as P

D = 768
ITERS = 2


eps = 0.01


def row_reduce(scores):
    local_max = jnp.max(scores, axis=1)
    top = lax.pmax(local_max, "col")
    total = lax.psum(jnp.sum(jnp.exp(scores - top[:, None]), axis=1), "col")
    return top + jnp.log(total)


def col_reduce(scores):
    local_max = jnp.max(scores, axis=0)
    top = lax.pmax(local_max, "row")
    total = lax.psum(jnp.sum(jnp.exp(scores - top[None, :]), axis=0), "row")
    return top + jnp.log(total)


def local(candidates, targets, target_domain, domain_counts):
    cand_block = lax.all_gather(candidates, "col", axis=0, tiled=True)
    domain_ids = jnp.arange(domain_counts.shape[0], dtype=jnp.int32)
    counts = domain_counts.astype(jnp.float32)
    onehot = (target_domain[:, None] == domain_ids[None, :]).astype(jnp.float32)
    local_weight = jnp.sum(onehot * counts[None, :], axis=1)
    tgt_block, weight = (
        lax.all_gather(targets, "row", axis=0, tiled=True),
        lax.all_gather(local_weight.astype(jnp.bfloat16), "row", axis=0, tiled=True).astype(
            local_weight.dtype
        ),
    )
    total_cols = tgt_block.shape[0] * lax.axis_size("col")
    logb = (
        jnp.log(weight / jnp.sum(counts))
        + jnp.log(jnp.float32(domain_counts.shape[0]))
        - jnp.log(jnp.float32(total_cols))
    )
    total_rows = cand_block.shape[0] * lax.axis_size("row")
    loga = -jnp.log(jnp.float32(total_rows))
    sqx = jnp.sum(jnp.square(cand_block.astype(jnp.float32)), axis=1)
    sqy = jnp.sum(jnp.square(tgt_block.astype(jnp.float32)), axis=1)
    cross = lax.dot_general(
        cand_block, tgt_block, (((1,), (1,)), ((), ())), preferred_element_type=jnp.float32
    )
    cost = (sqx[:, None] + sqy[None, :] - 2.0 * cross) / D
    tgt_pot = jnp.zeros(sqy.shape, jnp.float32)
    for it in range(ITERS):
        cand_pot = eps * loga - eps * row_reduce((tgt_pot[None, :] - cost) / eps)
        tgt_pot = eps * logb - eps * col_reduce((cand_pot[:, None] - cost) / eps)
    cand_pot = eps * loga - eps * row_reduce((tgt_pot[None, :] - cost) / eps)
    plan = jnp.exp((cand_pot[:, None] + tgt_pot[None, :] - cost) / eps - loga).astype(jnp.bfloat16)
    share = cand_block.shape[0] // lax.axis_size("col")
    partial_value = jnp.dot(plan, tgt_block, preferred_element_type=jnp.float32)
    summed = lax.psum(partial_value.astype(jnp.bfloat16), "col").astype(jnp.float32)
    projection = lax.dynamic_slice_in_dim(summed, lax.axis_index("col") * share, share, 0).astype(
        jnp.bfloat16
    )
    return (projection, cand_pot, tgt_pot)


def solution(mesh):
    placed = (P(("row", "col"), None), P(("col", "row"), None), P(("col", "row")), P())
    return jax.shard_map(
        local,
        mesh=mesh,
        in_specs=placed,
        out_specs=(P(("row", "col"), None), P("row"), P("col")),
        check_vma=False,
    )
```

profile of v0, /device:TPU:32, one launch (start us, length us, event | category | flops | bytes accessed | tf_op | source)
XLA Modules:
  0.0 705.3 jit_solution(1020448188829880788)
XLA Ops:
  7.2 0.7 all-gather.4.cloned.1.call-update
  7.9 0.7 all-gather.6.cloned.1.call-update
  9.4 0.7 select_reduce_fusion
  10.1 19.7 %all-gather = bf16[16,1,128]{2,1,0:T(2,128)(2,1)S(1)} all-gather(bf16[1,1,128]{2,1,0:T(2,128)(2,1)S(1)} %bitcast.12), channel_id=1, replica_groups=mesh['row'=16,'col'=16] {'row'}, dimensions={0}, use_global_device_ids=true | all-gather | bytes 4352 | tf_op jit(solution)/shard_map/all_gather | solution.py:35
  29.9 1.3 convert_reduce_fusion
  31.1 63.8 %all-gather.4.cloned.1.call-done = bf16[1024,768]{1,0:T(8,128)(2,1)} async-done(((bf16[64,768]{1,0:T(8,128)(2,1)}), bf16[1024,768]{1,0:T(8,128)(2,1)}) %all-gather.4.cloned.1.call-update) | async-done | bytes 1572880 | tf_op jit(solution)/shard_map/all_gather | solution.py:28
  94.9 1.8 multiply_reduce_fusion.1
  96.7 35.7 %all-gather.6.cloned.1.call-done = bf16[2048,768]{1,0:T(8,128)(2,1)} async-done(((bf16[128,768]{1,0:T(8,128)(2,1)}), bf16[2048,768]{1,0:T(8,128)(2,1)}) %all-gather.6.cloned.1.call-update) | async-done | bytes 3145744 | tf_op jit(solution)/shard_map/all_gather | solution.py:34
  132.4 2.6 multiply_reduce_fusion
  135.0 9.4 %fusion = (f32[1024]{0:T(1024)S(1)}, f32[1024,2048]{1,0:T(8,128)}) fusion(bf16[1024,768]{1,0:T(8,128)(2,1)} %all-gather.4.cloned.1.call-done, bf16[2048,768]{1,0:T(8,128)(2,1)} %all-gather.6.cloned.1.call-done, f32[2048]{0:T(1024)S(1)} %multiply_reduce_fusion, f32[1024]{0:T(1024)S(1)} %multiply_reduce_fusion.1), kind=kOutput, calls=%fused_computation.12 | convolution fusion | flops 3235904512 | bytes 13123584 | tf_op jit(solution)/shard_map/dot_general | solution.py:49
  144.4 39.8 %pmax.35 = f32[1024]{0:T(1024)S(1)} all-reduce(f32[1024]{0:T(1024)S(1)} %get-tuple-element.3), channel_id=1, replica_groups=mesh['row'=16,'col'=16] {'col'}, use_global_device_ids=true, to_apply=%region_5.0 | all-reduce | flops 1024 | bytes 8192 | tf_op jit(solution)/shard_map/pmax | solution.py:15
  184.2 4.5 exponential_reduce_fusion.4
  188.7 36.6 %psum.42 = f32[1024]{0:T(1024)S(1)} all-reduce(f32[1024]{0:T(1024)S(1)} %exponential_reduce_fusion.4), channel_id=1, replica_groups=mesh['row'=16,'col'=16] {'col'}, use_global_device_ids=true, to_apply=%region_7.0 | all-reduce | flops 1024 | bytes 8192 | tf_op jit(solution)/shard_map/psum | solution.py:16
  225.4 4.3 fusion.1
  229.7 27.6 %pmax.36 = f32[2048]{0:T(1024)S(1)} all-reduce(f32[2048]{0:T(1024)S(1)} %fusion.1), channel_id=1, replica_groups=mesh['row'=16,'col'=16] {'row'}, use_global_device_ids=true, to_apply=%region_9.0 | all-reduce | flops 2048 | bytes 16384 | tf_op jit(solution)/shard_map/pmax | solution.py:22
  257.3 4.5 exponential_reduce_fusion.3
  261.8 27.6 %psum.43 = f32[2048]{0:T(1024)S(1)} all-reduce(f32[2048]{0:T(1024)S(1)} %exponential_reduce_fusion.3), channel_id=1, replica_groups=mesh['row'=16,'col'=16] {'row'}, use_global_device_ids=true, to_apply=%region_11.0 | all-reduce | flops 2048 | bytes 16384 | tf_op jit(solution)/shard_map/psum | solution.py:23
  290.2 4.3 fusion.2
  294.5 40.1 %pmax.37 = f32[1024]{0:T(1024)S(1)} all-reduce(f32[1024]{0:T(1024)S(1)} %fusion.2), channel_id=1, replica_groups=mesh['row'=16,'col'=16] {'col'}, use_global_device_ids=true, to_apply=%region_13.0 | all-reduce | flops 1024 | bytes 8192 | tf_op jit(solution)/shard_map/pmax | solution.py:15
  334.6 4.5 exponential_reduce_fusion.2
  339.1 36.6 %psum.44 = f32[1024]{0:T(1024)S(1)} all-reduce(f32[1024]{0:T(1024)S(1)} %exponential_reduce_fusion.2), channel_id=1, replica_groups=mesh['row'=16,'col'=16] {'col'}, use_global_device_ids=true, to_apply=%region_15.0 | all-reduce | flops 1024 | bytes 8192 | tf_op jit(solution)/shard_map/psum | solution.py:16
  375.8 4.3 fusion.3
  380.0 27.8 %pmax.38 = f32[2048]{0:T(1024)S(1)} all-reduce(f32[2048]{0:T(1024)S(1)} %fusion.3), channel_id=1, replica_groups=mesh['row'=16,'col'=16] {'row'}, use_global_device_ids=true, to_apply=%region_17.0 | all-reduce | flops 2048 | bytes 16384 | tf_op jit(solution)/shard_map/pmax | solution.py:22
  407.9 4.5 exponential_reduce_fusion.1
  412.4 27.6 %psum.45 = f32[2048]{0:T(1024)S(1)} all-reduce(f32[2048]{0:T(1024)S(1)} %exponential_reduce_fusion.1), channel_id=1, replica_groups=mesh['row'=16,'col'=16] {'row'}, use_global_device_ids=true, to_apply=%region_19.0 | all-reduce | flops 2048 | bytes 16384 | tf_op jit(solution)/shard_map/psum | solution.py:23
  440.7 4.4 fusion.4
  445.2 40.1 %pmax.39 = f32[1024]{0:T(1024)S(1)} all-reduce(f32[1024]{0:T(1024)S(1)} %fusion.4), channel_id=1, replica_groups=mesh['row'=16,'col'=16] {'col'}, use_global_device_ids=true, to_apply=%region_21.0 | all-reduce | flops 1024 | bytes 8192 | tf_op jit(solution)/shard_map/pmax | solution.py:15
  485.3 4.5 exponential_reduce_fusion
  489.8 36.6 %psum.46 = f32[1024]{0:T(1024)S(1)} all-reduce(f32[1024]{0:T(1024)S(1)} %exponential_reduce_fusion), channel_id=1, replica_groups=mesh['row'=16,'col'=16] {'col'}, use_global_device_ids=true, to_apply=%region_23.0 | all-reduce | flops 1024 | bytes 8192 | tf_op jit(solution)/shard_map/psum | solution.py:16
  526.5 8.8 %fusion.10 = bf16[1024,768]{1,0:T(8,128)(2,1)} fusion(bf16[2048,768]{1,0:T(8,128)(2,1)S(1)} %copy-done, f32[1024,2048]{1,0:T(8,128)} %get-tuple-element.4, f32[1024]{0:T(1024)S(1)} %multiply_subtract_fusion.2, f32[2048]{0:T(1024)S(1)} %multiply_subtract_fusion), kind=kOutput, calls=%fused_computation.24 | convolution fusion | flops 3232497664 | bytes 13119488 | tf_op jit(solution)/shard_map/dot_general | solution.py:60
  535.3 161.9 %all-reduce.2.cloned.1.call-done = bf16[1024,768]{1,0:T(8,128)(2,1)} async-done(((bf16[1024,768]{1,0:T(8,128)(2,1)}), bf16[1024,768]{1,0:T(8,128)(2,1)}) %all-reduce.2.cloned.1.call-update) | async-done | bytes 1572880 | tf_op jit(solution)/shard_map/psum | solution.py:61
  697.3 1.5 convert_convert_fusion
  (16 shorter events, 2.2 us)
Async XLA Ops:
  7.2 87.8 %all-gather.4.cloned.1.call-start = ((), (), s32[]{:S(2)}) async-start(), calls=%async_computation | async-start | bytes 1671168 | tf_op jit(solution)/shard_map/all_gather | solution.py:28
  7.9 124.5 %all-gather.6.cloned.1.call-start = ((), (), s32[]{:S(2)}) async-start(), calls=%async_computation.1 | async-start | bytes 3342336 | tf_op jit(solution)/shard_map/all_gather | solution.py:34
  8.6 688.6 %all-reduce.2.cloned.1.call-start = ((), (), s32[]{:S(2)}) async-start(), calls=%async_computation.2 | async-start | bytes 3145728 | tf_op jit(solution)/shard_map/psum | solution.py:61
  440.7 85.8 %copy-start.1 = (f32[2048]{0:T(1024)}, f32[2048]{0:T(1024)S(1)}, u32[]{:S(2)}) copy-start(f32[2048]{0:T(1024)S(1)} %multiply_subtract_fusion) | copy-start | bytes 24580
  440.7 85.8 %copy-start = (bf16[2048,768]{1,0:T(8,128)(2,1)S(1)}, bf16[2048,768]{1,0:T(8,128)(2,1)}, u32[]{:S(2)}) copy-start(bf16[2048,768]{1,0:T(8,128)(2,1)} %all-gather.6.cloned.1.call-done) | copy-start | bytes 9437188
  526.5 8.8 %copy-start.2 = (f32[1024]{0:T(1024)}, f32[1024]{0:T(1024)S(1)}, u32[]{:S(2)}) copy-start(f32[1024]{0:T(1024)S(1)} %multiply_subtract_fusion.2) | copy-start | bytes 12292
Sparse Core Ops, SparseCore 0:
  10.6 84.2 all-gather.3
  96.8 35.6 all-gather.5
  535.5 161.7 all-reduce.1
where the time goes:
time: 707 us; the launch traced here: 705 us
  blocking collectives  361 us (51%)
  waiting for transfers between devices  263 us (37%)
  other arithmetic  49.7 us (7%)
  matrix products  18.2 us (3%)
  between operations  13.9 us (2%)
    psum x1, waiting for transfers between devices, local(): lax.psum(partial_value.astype(jnp.bfloat16), 'col').astype(jnp.float32)  162 us
    pmax x3, blocking collectives, row_reduce(): top = lax.pmax(local_max, 'col')  120 us
    psum x3, blocking collectives, row_reduce(): total = lax.psum(jnp.sum(jnp.exp(scores - top[:, None]), axis=1), 'col')  110 us
    all_gather x1, waiting for transfers between devices, local(): cand_block = lax.all_gather(candidates, 'col', axis=0, tiled=True)  63.8 us
    pmax x2, blocking collectives, col_reduce(): top = lax.pmax(local_max, 'row')  55.5 us
    psum x2, blocking collectives, col_reduce(): total = lax.psum(jnp.sum(jnp.exp(scores - top[None, :]), axis=0), 'row')  55.3 us
    all_gather x1, waiting for transfers between devices, local(): lax.all_gather(targets, 'row', axis=0, tiled=True)  35.7 us
    all_gather x1, blocking collectives, local(): lax.all_gather(local_weight.astype(jnp.bfloat16), 'row', axis=0, tiled=True)  19.7 us
  transfers between devices with their start and end apart: 3, of which 3 were waited for; matrix products, arithmetic and copies ran while one was open for 1% of the time, Pallas kernels for 0%

commit v1 on v0

v1 whole, which is shorter than its diff:
```python
import functools
import math

import jax
import jax.numpy as jnp
from jax import lax
from jax.experimental import pallas as pl
from jax.experimental.pallas import tpu as pltpu
from jax.sharding import Mesh, PartitionSpec as P

eps = 0.01
LOG2E = math.log2(math.e)
TO2 = LOG2E / eps

ROW = ("xl", "y", "core")
COL = ("z", "xh")
CG = ("xh", "xl", "y")
TG = ("core", "z")
RING = (0, -1, -2, -3, 1, 2, 3, 4)
LANE = 128
SUB = 64
BLK = 256
MIB = 1024 * 1024
VMEM_LIMIT = 30 * MIB


def spread(row):
    return jnp.broadcast_to(row, (LANE, LANE)).T


def fold_lanes(m, l):
    mt, lt = m.T, l.T
    top = jnp.max(mt, axis=0, keepdims=True)
    return top + jnp.log2(jnp.sum(lt * jnp.exp2(mt - top), axis=0, keepdims=True))


def merge(parts):
    top = jnp.max(parts, axis=0)
    return top + jnp.log2(jnp.sum(jnp.exp2(parts - top[None]), axis=0))


def copies(out_ref, at, value):
    for d in range(out_ref.shape[0]):
        out_ref[d, pl.ds(at, 1), :] = value


def spread_kernel(x_ref, out_ref, sems):
    started = []
    for d in range(out_ref.shape[0]):
        copy = pltpu.make_async_copy(x_ref, out_ref.at[d], sems.at[d])
        copy.start()
        started.append(copy)
    for copy in started:
        copy.wait()


def norms(scale, x_ref, out_ref):
    for r in range(0, x_ref.shape[0], LANE):
        acc = jnp.zeros((LANE, LANE), jnp.float32)
        for k in range(0, x_ref.shape[1], LANE):
            x = x_ref[pl.ds(r, LANE), pl.ds(k, LANE)].astype(jnp.float32)
            acc = acc + x * x
        total = jnp.sum(acc, axis=1, keepdims=True) * scale
        out_ref[pl.ds(r, LANE), :] = jnp.broadcast_to(total, (LANE, LANE))


def half_cost(scale, x_ref, sqx_ref, y_ref, c_ref, m_ref, l_ref):
    rows, half = c_ref.shape
    tiles = half // LANE
    sqy = []
    for t in range(tiles):
        acc = jnp.zeros((LANE, LANE), jnp.float32)
        for k in range(0, y_ref.shape[1], LANE):
            y = y_ref[pl.ds(t * LANE, LANE), pl.ds(k, LANE)].astype(jnp.float32)
            acc = acc + y * y
        sqy.append(jnp.sum(acc.T, axis=0, keepdims=True) * scale)
    wide = 512
    for b in range(0, rows, BLK):
        x = x_ref[pl.ds(b, BLK), :]
        for at in range(0, half, wide):
            cross = lax.dot_general(
                x, y_ref[pl.ds(at, wide), :], (((1,), (1,)), ((), ())), preferred_element_type=jnp.float32
            )
            for r in range(0, BLK, SUB):
                here = pl.ds(b + r, SUB)
                sqx = sqx_ref[here, :]
                low = l_ref[here, :] if at else None
                for k in range(wide // LANE):
                    t = at // LANE + k
                    part = cross[r : r + SUB, k * LANE : (k + 1) * LANE]
                    cost = (sqx + sqy[t]) - (2.0 * scale) * part
                    c_ref[here, pl.ds(t * LANE, LANE)] = cost
                    low = cost if low is None else jnp.minimum(low, cost)
                l_ref[here, :] = low
        for r in range(b, b + BLK, SUB):
            here = pl.ds(r, SUB)
            low = l_ref[here, :]
            l = jnp.zeros((SUB, LANE), jnp.float32)
            for t in range(tiles):
                l = l + jnp.exp2(low - c_ref[here, pl.ds(t * LANE, LANE)])
            m_ref[here, :] = -low
            l_ref[here, :] = l


def first_cost(scale, x_ref, y_ref, c_ref, m_ref, l_ref, sqx_ref):
    norms(scale, x_ref, sqx_ref)
    half_cost(scale, x_ref, sqx_ref, y_ref, c_ref, m_ref, l_ref)


def place(tile):
    n = len(RING)
    core = lax.rem(tile // n + lax.axis_index("core"), 2)
    return core * n + lax.rem(lax.axis_index("z") + RING[tile % n] + n, n)


def second_cost(scale, x_ref, sqx_ref, y_ref, m0_ref, l0_ref, c_ref, out_ref, m_ref, l_ref):
    half_cost(scale, x_ref, sqx_ref, y_ref, c_ref, m_ref, l_ref)
    for k in range(c_ref.shape[0] // LANE):
        here = pl.ds(k * LANE, LANE)
        m0, m1 = m0_ref[here, :], m_ref[here, :]
        m = jnp.maximum(m0, m1)
        l = l0_ref[here, :] * jnp.exp2(m0 - m) + l_ref[here, :] * jnp.exp2(m1 - m)
        copies(out_ref, k, fold_lanes(m, l))


def col_kernel(log2a, parts_ref, ca_ref, cb_ref, *refs):
    *logb_ref, out_ref, u_ref = refs
    rows, half = ca_ref.shape
    total = 2 * half // LANE
    if logb_ref:
        copies(out_ref, total, logb_ref[0][...])
        for k in range(total + 1, out_ref.shape[1]):
            copies(out_ref, k, jnp.zeros((1, LANE), jnp.float32))
    u = log2a - merge(parts_ref[...])
    for k in range(rows // LANE):
        u_ref[pl.ds(k * LANE, LANE), :] = spread(u[k : k + 1, :])
    sub, group = 32, 4
    for h, c_ref in enumerate((ca_ref, cb_ref)):
        for k0 in range(0, half // LANE, group):
            ks = range(k0, k0 + group)

            def score(r, k):
                return u_ref[pl.ds(r, sub), :] - c_ref[pl.ds(r, sub), pl.ds(k * LANE, LANE)]

            def top_step(i, m):
                r = pl.multiple_of(i * sub, sub)
                return tuple(jnp.maximum(a, score(r, k)) for a, k in zip(m, ks))

            def sum_step(m, i, l):
                r = pl.multiple_of(i * sub, sub)
                return tuple(a + jnp.exp2(score(r, k) - b) for a, b, k in zip(l, m, ks))

            m = lax.fori_loop(1, rows // sub, top_step, tuple(score(0, k) for k in ks), unroll=4)
            zero = jnp.zeros((sub, LANE), jnp.float32)
            l = lax.fori_loop(
                0, rows // sub, functools.partial(sum_step, m), (zero,) * group, unroll=4
            )
            for a, b, k in zip(l, m, ks):
                top = jnp.max(b, axis=0, keepdims=True)
                e = top + jnp.log2(jnp.sum(a * jnp.exp2(b - top), axis=0, keepdims=True))
                copies(out_ref, place(h * (total // 2) + k), e)


def tgt_pot(parts, logb_ref, v_ref, pot_ref):
    pot_ref[...] = logb_ref[...] - merge(parts)
    for t in range(v_ref.shape[0]):
        v_ref[pl.ds(t, 1), :] = pot_ref[pl.ds(place(t), 1), :]


def scores(v_ref, ca_ref, cb_ref, here):
    tiles = ca_ref.shape[1] // LANE

    def score(t):
        ref = ca_ref if t < tiles else cb_ref
        return v_ref[pl.ds(t, 1), :] - ref[here, pl.ds((t % tiles) * LANE, LANE)]

    return score, 2 * tiles


def row_kernel(parts_ref, ca_ref, cb_ref, out_ref, logb_ref, v_ref, pot_ref, m_ref, l_ref):
    rows = ca_ref.shape[0]
    total = v_ref.shape[0]
    for d in range(total):
        logb_ref[pl.ds(d, 1), :] = parts_ref[d, pl.ds(total, 1), :]
    tgt_pot(parts_ref[:, pl.ds(0, total), :], logb_ref, v_ref, pot_ref)

    def body(i, carry):
        here = pl.ds(pl.multiple_of(i * LANE, LANE), LANE)
        score, tiles = scores(v_ref, ca_ref, cb_ref, here)
        m = score(0)
        for t in range(1, tiles):
            m = jnp.maximum(m, score(t))
        l = jnp.zeros((LANE, LANE), jnp.float32)
        for t in range(tiles):
            l = l + jnp.exp2(score(t) - m)
        m_ref[here, :] = m
        l_ref[here, :] = l
        return carry

    lax.fori_loop(0, rows // LANE, body, 0)
    for k in range(rows // LANE):
        here = pl.ds(k * LANE, LANE)
        copies(out_ref, k, fold_lanes(m_ref[here, :], l_ref[here, :]))


def plan_kernel(parts_ref, logb_ref, ca_ref, cb_ref, ya_ref, yb_ref, out_ref, p_ref, v_ref, pot_ref, plan_ref, held_ref, sems):
    rows, half = ca_ref.shape
    tgt_pot(parts_ref[...], logb_ref, v_ref, pot_ref)
    first = 2 * rows // LANE
    n = pot_ref.shape[0] // 2
    for h in range(2):
        copies(out_ref, first + h, pot_ref[pl.ds(lax.axis_index("z") + h * n, 1), :])
    for k in range(first + 2, out_ref.shape[1]):
        copies(out_ref, k, jnp.zeros((1, LANE), jnp.float32))

    leaving = []
    for k in range(rows // LANE):
        here = pl.ds(k * LANE, LANE)
        score, tiles = scores(v_ref, ca_ref, cb_ref, here)
        m = score(0)
        for t in range(1, tiles):
            m = jnp.maximum(m, score(t))
        m = jnp.broadcast_to(jnp.max(m, axis=1, keepdims=True), (LANE, LANE))
        l = jnp.zeros((LANE, LANE), jnp.float32)
        for t in range(tiles):
            p = jnp.exp2(score(t) - m)
            l = l + p
            plan_ref[here, pl.ds(t * LANE, LANE)] = p.astype(jnp.bfloat16)
        m = m.T[:1, :]
        l = jnp.sum(l.T, axis=0, keepdims=True)
        copies(out_ref, k, m + jnp.log2(l))
        copies(out_ref, rows // LANE + k, m)
        if (k + 1) * LANE % BLK == 0:
            here = pl.ds((k + 1) * LANE - BLK, BLK)
            total = jnp.dot(plan_ref[here, pl.ds(0, half)], ya_ref[...], preferred_element_type=jnp.float32)
            total = total + jnp.dot(
                plan_ref[here, pl.ds(half, half)], yb_ref[...], preferred_element_type=jnp.float32
            )
            held_ref[here, :] = total.astype(jnp.bfloat16)
            copy = pltpu.make_async_copy(held_ref.at[here], p_ref.at[here], sems.at[k * LANE // BLK])
            copy.start()
            leaving.append(copy)
    for copy in leaving:
        copy.wait()


def last_kernel(log2a, share, parts_ref, gain_ref, cand_ref, tgt_ref):
    top = share * lax.axis_size(CG) // LANE
    per = LANE // share
    per_xh = top // lax.axis_size("xh")
    mine = lax.axis_index(("xl", "y"))
    lane = lax.broadcasted_iota(jnp.int32, (1, LANE), 1) // share
    lse = merge(parts_ref[:, pl.ds(0, top), :])
    cand_ref[...] = jnp.zeros(cand_ref.shape, jnp.float32)
    row_of = lax.broadcasted_iota(jnp.int32, lse.shape, 0)

    def row(value, at):
        return jnp.sum(jnp.where(row_of == at, value, 0.0), axis=0, keepdims=True)

    def shifted(value, to, at):
        out = jnp.zeros_like(value)
        for off in range(per):
            moved = pltpu.roll(value, ((to - off) % per) * share, 1) if (to - off) % per else value
            out = jnp.where(at == off, moved, out)
        return out

    pieces = jnp.zeros((1, LANE), jnp.float32)
    for h in range(lax.axis_size("xh")):
        value = shifted(row(lse, h * per_xh + mine // per), h, lax.rem(mine, per))
        pieces = jnp.where(lane == h, value, pieces)
    cand_ref[pl.ds(lax.axis_index("z"), 1), :] = (log2a - pieces) / TO2

    me = lax.axis_index(CG)
    own = parts_ref[:, pl.ds(top + me // per, 1), :].reshape(parts_ref.shape[0], LANE)
    gain_ref[...] = shifted(jnp.exp2(own - row(lse, me // per)), 0, lax.rem(me, per))

    n = lax.axis_size(("xl", "y"))
    for k in range(n):
        pair = parts_ref[lax.axis_index("xh") * n + k, pl.ds(2 * top, 2), :]
        tgt_ref[pl.ds(2 * k, 2), :] = pair / TO2


VMEM = pl.BlockSpec(memory_space=pltpu.VMEM)
HBM = pl.BlockSpec(memory_space=pltpu.HBM)


def local(candidates, targets, target_domain, domain_counts):
    f32, bf16 = jnp.float32, jnp.bfloat16
    width = candidates.shape[1]
    plane = lax.axis_size(CG)
    pairs = lax.axis_size(TG)
    depth = lax.axis_size("z")
    share = candidates.shape[0]
    rows = share * plane
    half = targets.shape[0] * depth
    cols = 2 * half
    total_rows = rows * pairs
    total_cols = cols * plane

    def run(kernel, args, outs, scratch=(), special=()):
        special = dict(special)
        return pl.pallas_call(
            kernel,
            in_specs=[special.get(i, VMEM) for i in range(len(args))],
            out_specs=[o[2] if len(o) > 2 else VMEM for o in outs],
            out_shape=[(pltpu.HBM if len(o) > 2 else jax.ShapeDtypeStruct)(o[0], o[1]) for o in outs],
            scratch_shapes=[pltpu.VMEM(*v) if isinstance(v, tuple) else v for v in scratch],
            compiler_params=pltpu.CompilerParams(vmem_limit_bytes=VMEM_LIMIT),
            cost_estimate=pl.CostEstimate(flops=rows * cols * width, bytes_accessed=4 * rows * cols, transcendentals=rows * cols),
        )(*[pltpu.with_memory_space_constraint(a, pltpu.HBM) if special.get(i) is HBM else a for i, a in enumerate(args)])

    def shift(block, by):
        return lax.ppermute(block, "z", [(i, (i + by) % depth) for i in range(depth)])

    (x,) = run(
        spread_kernel,
        (candidates,),
        [((plane, share, width), bf16, HBM)],
        [pltpu.SemaphoreType.DMA((plane,))],
    )
    x = lax.all_to_all(x, CG, 0, 0, tiled=True).reshape(rows, width)
    up, down = [targets], [targets]
    for _ in range(depth // 2 - 1):
        up.append(shift(up[-1], 1))
        down.append(shift(down[-1], -1))
    mid = targets.shape[0] // 2
    ends = [shift(up[-1][:mid], 1), shift(down[-1][mid:], -1)]
    ya = jnp.concatenate(up + down[1:] + ends, axis=0)
    counts = domain_counts.astype(f32)
    domains = jnp.arange(domain_counts.shape[0], dtype=jnp.int32)
    weight = jnp.sum(jnp.where(target_domain[:, None] == domains[None, :], counts[None, :], 0.0), axis=1)
    logb = jnp.log2(weight / jnp.sum(counts)) + (
        math.log2(domain_counts.shape[0]) - math.log2(total_cols)
    )
    scale = TO2 / width
    ya, x, logb = lax.optimization_barrier((ya, x, logb[None, :]))
    yb = lax.ppermute(ya, "core", [(0, 1), (1, 0)])

    log2a = -math.log2(total_rows)
    row_shape = ((plane, rows // LANE, LANE), f32)
    col_shape = ((pairs, cols // LANE, LANE), f32)
    wide_shape = ((pairs, cols // LANE + 8, LANE), f32)
    last_shape = ((plane, 2 * rows // LANE + 8, LANE), f32)
    stat = ((rows, LANE), f32)
    vec = ((cols // LANE, LANE), f32)
    chalf = ((rows, half), f32)
    ca, m, l, sqx = run(functools.partial(first_cost, scale), (x, ya), [chalf, stat, stat, stat])
    cb, out = run(
        functools.partial(second_cost, scale), (x, sqx, yb, m, l), [chalf, row_shape], [stat, stat]
    )

    def columns(out, shape, *extra):
        parts = lax.all_to_all(out, CG, 0, 0, tiled=True)
        (out,) = run(functools.partial(col_kernel, log2a), (parts, ca, cb, *extra), [shape], [stat])
        return lax.all_to_all(out, TG, 0, 0, tiled=True)

    out, logb = run(
        row_kernel, (columns(out, wide_shape, logb), ca, cb), [row_shape, vec], [vec, vec, stat, stat]
    )
    out, partial = run(
        plan_kernel,
        (columns(out, col_shape), logb, ca, cb, ya, yb),
        [last_shape, ((rows, width), bf16, HBM)],
        [vec, vec, ((rows, cols), bf16), ((rows, width), bf16), pltpu.SemaphoreType.DMA((rows // BLK,))],
    )
    parts = lax.all_to_all(out, CG, 0, 0, tiled=True)
    moved = lax.all_to_all(partial.reshape(plane, share, width), CG, 0, 0, tiled=True)
    gain, cand, tgt = run(
        functools.partial(last_kernel, log2a, share),
        (parts,),
        [((plane, LANE), f32), ((depth, LANE), f32), vec],
    )
    projection = jnp.sum(moved.astype(f32) * gain[:, :share, None], axis=0).astype(bf16)
    for bit in (1, 2, 4):
        cand = cand + lax.ppermute(cand, "z", [(i, i ^ bit) for i in range(depth)])
    return projection, cand.reshape(-1), tgt.reshape(-1)


def solution(mesh):
    fine = Mesh(mesh.devices.reshape(2, -1, 2, mesh.shape["col"] // 2, 2), ROW + COL)
    tgt = P(COL + ROW)
    return jax.shard_map(
        local,
        mesh=fine,
        in_specs=(P(ROW + COL, None), P(COL + ROW, None), tgt, P()),
        out_specs=(P(ROW + COL, None), P(ROW), P(COL)),
        check_vma=False,
    )
```

time: 707 us -> 148 us (0.21)
  blocking collectives: 361 us -> 65.8 us
  waiting for transfers between devices: 263 us -> 29.5 us
  other arithmetic: 49.7 us -> 2.96 us
  starting transfers between devices: 0.11 us -> 25.9 us
  Pallas kernels: 0 us -> 20.6 us
  matrix products: 18.2 us -> 0 us
  between operations: 13.9 us -> 0.84 us
    pmax x5 -> x0, blocking collectives: 176 us -> none  [the longest x3 120 us: row_reduce(): top = lax.pmax(local_max, 'col')]
    psum x5 -> x0, blocking collectives: 165 us -> none  [the longest x3 110 us: row_reduce(): total = lax.psum(jnp.sum(jnp.exp(scores - top[:, None]), axis=1), 'col')]
    psum x1 -> x0, waiting for transfers between devices: 162 us -> none  [local(): lax.psum(partial_value.astype(jnp.bfloat16), 'col').astype(jnp.float32)]
    all_gather x2 -> x0, waiting for transfers between devices: 99.5 us -> none  [the longest x1 63.8 us: local(): cand_block = lax.all_gather(candidates, 'col', axis=0, tiled=True)]
    all_to_all x0 -> x5, blocking collectives: none -> 65.8 us  [the longest x2 29.7 us: columns(): return lax.all_to_all(out, TG, 0, 0, tiled=True)]
    reduce_sum x8 -> x2, other arithmetic: 27.6 us -> 1.1 us  [the longest x1 1.01 us: local(): jnp.sum(moved.astype(f32) * gain[:, :share, None], axis=0).astype(bf16)]
    ppermute x0 -> x12, waiting for transfers between devices: none -> 23.8 us  [the longest x3 12.8 us: local(): cand = cand + lax.ppermute(cand, 'z', [(i, i ^ bit) for i in range(depth)])]
    pallas_call x0 -> x8, Pallas kernels: none -> 20.6 us  [run(): pl.pallas_call(kernel, in_specs=[special.get(i, VMEM) for i in range(len(...]
  transfers between devices with their start and end apart: 3 -> 14, of which waited for: 3 -> 12; matrix products, arithmetic and copies ran while one was open for 1% -> 2% of each run, Pallas kernels for 0% -> 3%
where the time goes in v1:
time: 148 us
  blocking collectives  65.8 us (44%)
  waiting for transfers between devices  29.5 us (20%)
  starting transfers between devices  25.9 us (18%)
  Pallas kernels  20.6 us (14%)
  other arithmetic  2.96 us (2%)
  local copies, waits for them, and re-layouts  1.97 us (1%)
    all_to_all x2, blocking collectives, columns(): return lax.all_to_all(out, TG, 0, 0, tiled=True)  29.7 us
    all_to_all x2, blocking collectives, columns(): parts = lax.all_to_all(out, CG, 0, 0, tiled=True)  24.7 us
    pallas_call x8, Pallas kernels, run(): pl.pallas_call(kernel, in_specs=[special.get(i, VMEM) for i in range(len(...  20.6 us
    ppermute x3, waiting for transfers between devices, local(): cand = cand + lax.ppermute(cand, 'z', [(i, i ^ bit) for i in range(depth)])  12.8 us
    ppermute x8, starting transfers between devices, shift(): lax.ppermute(block, 'z', [(i, (i + by) % depth) for i in range(depth)])  12.2 us
    all_to_all x1, blocking collectives, local(): parts = lax.all_to_all(out, CG, 0, 0, tiled=True)  11.3 us
    ppermute x8, waiting for transfers between devices, shift(): lax.ppermute(block, 'z', [(i, (i + by) % depth) for i in range(depth)])  9.95 us
    all_to_all x1, starting transfers between devices, local(): x = lax.all_to_all(x, CG, 0, 0, tiled=True).reshape(rows, width)  7.18 us
  transfers between devices with their start and end apart: 14, of which 12 were waited for; matrix products, arithmetic and copies ran while one was open for 2% of the time, Pallas kernels for 3%

profile of v1, /device:TPU:32, one launch (start us, length us, event | category | flops | bytes accessed | tf_op | source)
XLA Modules:
  0.0 147.6 jit_solution(14969486576756360702)
XLA Ops:
  0.6 2.0 %collective-permute-start = (bf16[128,768]{1,0:T(8,128)(2,1)}, bf16[128,768]{1,0:T(8,128)(2,1)}, u32[]{:S(2)}, u32[]{:S(2)}) collective-permute-start(bf16[128,768]{1,0:T(8,128)(2,1)} %param.5), channel_id=1, source_target_pairs={{0,2},{2,4},{4,6},{6,8},{8,10},{10,12},{12,14},{14,0},{1,3},{3,5},... | collective-permute-start | bytes 589832 | tf_op jit(solution)/shard_map/ppermute | solution.py:313
  2.7 0.9 copy-done
  3.6 1.3 shard_map.67
  5.0 7.2 %all-to-all-start = ((bf16[16,64,768]{2,1,0:T(8,128)(2,1)}), bf16[16,64,768]{2,1,0:T(8,128)(2,1)S(1)}, u32[]{:S(2)}, u32[]{:S(2)}) async-start(bf16[16,64,768]{2,1,0:T(8,128)(2,1)} %shard_map.67), calls=%async_computation | async-start | bytes 3145728 | tf_op jit(solution)/shard_map/all_to_all | solution.py:321
  12.9 2.0 %collective-permute-start.1 = (bf16[128,768]{1,0:T(8,128)(2,1)}, bf16[128,768]{1,0:T(8,128)(2,1)S(1)}, u32[]{:S(2)}, u32[]{:S(2)}) collective-permute-start(bf16[128,768]{1,0:T(8,128)(2,1)} %collective-permute-done), channel_id=1, source_target_pairs={{0,2},{2,4},{4,6},{6,8},{8,10},{10,12},{12,14},{14,0},{1,3},{3,5},... | collective-permute-start | bytes 589832 | tf_op jit(solution)/shard_map/ppermute | solution.py:313
  14.9 2.2 %collective-permute-start.4 = (bf16[128,768]{1,0:T(8,128)(2,1)S(1)}, bf16[128,768]{1,0:T(8,128)(2,1)S(1)}, u32[]{:S(2)}, u32[]{:S(2)}) collective-permute-start(bf16[128,768]{1,0:T(8,128)(2,1)S(1)} %collective-permute-done.3), channel_id=1, source_target_pairs={{0,14},{2,0},{4,2},{6,4},{8,6},{10,8},{12,10},{14,12},{1,15},{3,1}... | collective-permute-start | bytes 589832 | tf_op jit(solution)/shard_map/ppermute | solution.py:313
  17.8 3.8 %collective-permute-done.1 = bf16[128,768]{1,0:T(8,128)(2,1)S(1)} collective-permute-done((bf16[128,768]{1,0:T(8,128)(2,1)}, bf16[128,768]{1,0:T(8,128)(2,1)S(1)}, u32[]{:S(2)}, u32[]{:S(2)}) %collective-permute-start.1) | collective-permute-done | bytes 196640 | tf_op jit(solution)/shard_map/ppermute | solution.py:313
  22.0 2.5 %collective-permute-start.5 = (bf16[128,768]{1,0:T(8,128)(2,1)S(1)}, bf16[128,768]{1,0:T(8,128)(2,1)S(1)}, u32[]{:S(2)}, u32[]{:S(2)}) collective-permute-start(bf16[128,768]{1,0:T(8,128)(2,1)S(1)} %collective-permute-done.4), channel_id=1, source_target_pairs={{0,14},{2,0},{4,2},{6,4},{8,6},{10,8},{12,10},{14,12},{1,15},{3,1}... | collective-permute-start | bytes 589832 | tf_op jit(solution)/shard_map/ppermute | solution.py:313
  24.6 0.9 constant_dynamic-update-slice_fusion.7
  25.5 2.7 %collective-permute-done.2 = bf16[128,768]{1,0:T(8,128)(2,1)S(1)} collective-permute-done((bf16[128,768]{1,0:T(8,128)(2,1)S(1)}, bf16[128,768]{1,0:T(8,128)(2,1)S(1)}, u32[]{:S(2)}, u32[]{:S(2)}) %collective-permute-start.2) | collective-permute-done | bytes 196640 | tf_op jit(solution)/shard_map/ppermute | solution.py:313
  28.6 3.0 %collective-permute-start.7 = (bf16[64,768]{1,0:T(8,128)(2,1)S(1)}, bf16[64,768]{1,0:T(8,128)(2,1)S(1)}, u32[]{:S(2)}, u32[]{:S(2)}) collective-permute-start(bf16[64,768]{1,0:T(8,128)(2,1)S(1)} %slice.13), channel_id=1, source_target_pairs={{0,14},{2,0},{4,2},{6,4},{8,6},{10,8},{12,10},{14,12},{1,15},{3,1}... | collective-permute-start | bytes 294920 | tf_op jit(solution)/shard_map/ppermute | solution.py:313
  31.7 2.4 %collective-permute-done.6 = bf16[64,768]{1,0:T(8,128)(2,1)S(1)} collective-permute-done((bf16[64,768]{1,0:T(8,128)(2,1)S(1)}, bf16[64,768]{1,0:T(8,128)(2,1)S(1)}, u32[]{:S(2)}, u32[]{:S(2)}) %collective-permute-start.6) | collective-permute-done | bytes 98336 | tf_op jit(solution)/shard_map/ppermute | solution.py:313
  35.6 2.4 %shard_map.68 = (f32[1024,1024]{1,0:T(8,128)S(1)}, f32[1024,128]{1,0:T(8,128)S(1)}, f32[1024,128]{1,0:T(8,128)S(1)}, f32[1024,128]{1,0:T(8,128)S(1)}) custom-call(bf16[1024,768]{1,0:T(8,128)(2,1)S(1)} %bitcast.8, bf16[1024,768]{1,0:T(8,128)(2,1)S(1)} %constant_dynamic-update-slice_fusion.y_ref.ya_ref), custom_call_target="tpu_custom_call" | custom-call | flops 1610612736 | bytes 8388608 | tf_op jit(solution)/shard_map/pallas_call | solution.py:302
  38.0 1.0 collective-permute-done.8.y_ref.yb_ref
  39.0 2.5 %shard_map.69 = (f32[1024,1024]{1,0:T(8,128)S(1)}, f32[16,8,128]{2,1,0:T(8,128)S(1)}) custom-call(bf16[1024,768]{1,0:T(8,128)(2,1)S(1)} %bitcast.9, f32[1024,128]{1,0:T(8,128)S(1)} %get-tuple-element.21.sqx_ref, bf16[1024,768]{1,0:T(8,128)(2,1)S(1)} %collective-permute-done.8.y_ref.yb_ref, f32[1024,128]{1,0:T(8,128)S(1)} %get-tuple-element.22.m0_ref, ...), custom_call_target="tpu_custom_call" | custom-call | flops 1610612736 | bytes 8388608 | tf_op jit(solution)/shard_map/pallas_call | solution.py:302
  41.5 13.8 %all_to_all.35.parts_ref = f32[16,8,128]{2,1,0:T(8,128)S(1)} all-to-all(f32[16,8,128]{2,1,0:T(8,128)S(1)} %get-tuple-element.24), channel_id=1, replica_groups=mesh['xl'=2,'y'=4,'core'=2,'z'=8,'xh'=2] {'xh','xl','y'}, dimensions={0} | all-to-all | bytes 131072 | tf_op jit(solution)/shard_map/all_to_all | solution.py:353
  55.3 2.7 %shard_map.70 = f32[16,24,128]{2,1,0:T(8,128)S(1)} custom-call(f32[16,8,128]{2,1,0:T(8,128)S(1)} %all_to_all.35.parts_ref, f32[1024,1024]{1,0:T(8,128)S(1)} %get-tuple-element.25.ca_ref, f32[1024,1024]{1,0:T(8,128)S(1)} %get-tuple-element.26.cb_ref, f32[1,128]{1,0:T(1,128)S(1)} %add_bitcast_fusion.1.refs_0_), custom_call_target="tpu_custom_call" | custom-call | flops 1610612736 | bytes 8388608 | tf_op jit(solution)/shard_map/pallas_call | solution.py:302
  58.0 18.1 %all_to_all.36.parts_ref = f32[16,24,128]{2,1,0:T(8,128)S(1)} all-to-all(f32[16,24,128]{2,1,0:T(8,128)S(1)} %shard_map.70), channel_id=1, replica_groups=mesh['xl'=2,'y'=4,'core'=2,'z'=8,'xh'=2] {'core','z'}, dimensions={0} | all-to-all | bytes 393216 | tf_op jit(solution)/shard_map/all_to_all | solution.py:355
  76.2 2.4 %shard_map.71 = (f32[16,8,128]{2,1,0:T(8,128)S(1)}, f32[16,128]{1,0:T(8,128)S(1)}) custom-call(f32[16,24,128]{2,1,0:T(8,128)S(1)} %all_to_all.36.parts_ref, f32[1024,1024]{1,0:T(8,128)S(1)} %get-tuple-element.25.ca_ref, f32[1024,1024]{1,0:T(8,128)S(1)} %get-tuple-element.26.cb_ref), custom_call_target="tpu_custom_call" | custom-call | flops 1610612736 | bytes 8388608 | tf_op jit(solution)/shard_map/pallas_call | solution.py:302
  78.5 10.9 %all_to_all.37.parts_ref = f32[16,8,128]{2,1,0:T(8,128)S(1)} all-to-all(f32[16,8,128]{2,1,0:T(8,128)S(1)} %get-tuple-element.28), channel_id=1, replica_groups=mesh['xl'=2,'y'=4,'core'=2,'z'=8,'xh'=2] {'xh','xl','y'}, dimensions={0} | all-to-all | bytes 131072 | tf_op jit(solution)/shard_map/all_to_all | solution.py:353
  89.4 2.7 %shard_map.72 = f32[16,16,128]{2,1,0:T(8,128)S(1)} custom-call(f32[16,8,128]{2,1,0:T(8,128)S(1)} %all_to_all.37.parts_ref, f32[1024,1024]{1,0:T(8,128)S(1)} %get-tuple-element.25.ca_ref, f32[1024,1024]{1,0:T(8,128)S(1)} %get-tuple-element.26.cb_ref), custom_call_target="tpu_custom_call" | custom-call | flops 1610612736 | bytes 8388608 | tf_op jit(solution)/shard_map/pallas_call | solution.py:302
  92.1 11.6 %all_to_all.38.parts_ref = f32[16,16,128]{2,1,0:T(8,128)S(1)} all-to-all(f32[16,16,128]{2,1,0:T(8,128)S(1)} %shard_map.72), channel_id=1, replica_groups=mesh['xl'=2,'y'=4,'core'=2,'z'=8,'xh'=2] {'core','z'}, dimensions={0} | all-to-all | bytes 262144 | tf_op jit(solution)/shard_map/all_to_all | solution.py:355
  103.7 6.0 %shard_map.73 = (f32[16,24,128]{2,1,0:T(8,128)S(1)}, bf16[1024,768]{1,0:T(8,128)(2,1)}) custom-call(f32[16,16,128]{2,1,0:T(8,128)S(1)} %all_to_all.38.parts_ref, f32[16,128]{1,0:T(8,128)S(1)} %get-tuple-element.29.logb_ref, f32[1024,1024]{1,0:T(8,128)S(1)} %get-tuple-element.25.ca_ref, f32[1024,1024]{1,0:T(8,128)S(1)} %get-tuple-element.26.cb_ref, ...), custom_call_target="tpu_custom_call" | custom-call | flops 1610612736 | bytes 8388608 | tf_op jit(solution)/shard_map/pallas_call | solution.py:302
  109.7 11.3 %all_to_all.39.parts_ref = f32[16,24,128]{2,1,0:T(8,128)S(1)} all-to-all(f32[16,24,128]{2,1,0:T(8,128)S(1)} %get-tuple-element.31), channel_id=1, replica_groups=mesh['xl'=2,'y'=4,'core'=2,'z'=8,'xh'=2] {'xh','xl','y'}, dimensions={0} | all-to-all | bytes 393216 | tf_op jit(solution)/shard_map/all_to_all | solution.py:366
  121.0 3.7 %all-to-all-start.5 = ((bf16[16,64,768]{2,1,0:T(8,128)(2,1)}), bf16[16,64,768]{2,1,0:T(8,128)(2,1)S(1)}, u32[]{:S(2)}, u32[]{:S(2)}) async-start(bf16[16,64,768]{2,1,0:T(8,128)(2,1)} %bitcast.11), calls=%async_computation.5 | async-start | bytes 3145728 | tf_op jit(solution)/shard_map/all_to_all | solution.py:367
  125.8 3.3 %collective-permute-done.9 = f32[8,128]{1,0:T(8,128)S(1)} collective-permute-done((f32[8,128]{1,0:T(8,128)S(1)}, f32[8,128]{1,0:T(8,128)S(1)}, u32[]{:S(2)}, u32[]{:S(2)}) %collective-permute-start.9) | collective-permute-done | bytes 4128 | tf_op jit(solution)/shard_map/ppermute | solution.py:375
  129.0 0.9 collective-permute-start.10
  129.9 3.6 %collective-permute-done.10 = f32[8,128]{1,0:T(8,128)S(1)} collective-permute-done((f32[8,128]{1,0:T(8,128)S(1)}, f32[8,128]{1,0:T(8,128)S(1)}, u32[]{:S(2)}, u32[]{:S(2)}) %collective-permute-start.10) | collective-permute-done | bytes 4128 | tf_op jit(solution)/shard_map/ppermute | solution.py:375
  133.5 1.5 %collective-permute-start.11 = (f32[8,128]{1,0:T(8,128)S(1)}, f32[8,128]{1,0:T(8,128)S(1)}, u32[]{:S(2)}, u32[]{:S(2)}) collective-permute-start(f32[8,128]{1,0:T(8,128)S(1)} %add.29), channel_id=1, source_target_pairs={{0,8},{2,10},{4,12},{6,14},{8,0},{10,2},{12,4},{14,6},{1,9},{3,11}... | collective-permute-start | bytes 12296 | tf_op jit(solution)/shard_map/ppermute | solution.py:375
  135.0 6.0 %collective-permute-done.11 = f32[8,128]{1,0:T(8,128)S(1)} collective-permute-done((f32[8,128]{1,0:T(8,128)S(1)}, f32[8,128]{1,0:T(8,128)S(1)}, u32[]{:S(2)}, u32[]{:S(2)}) %collective-permute-start.11) | collective-permute-done | bytes 4128 | tf_op jit(solution)/shard_map/ppermute | solution.py:375
  141.6 4.9 %all-to-all-done.5 = bf16[16,64,768]{2,1,0:T(8,128)(2,1)S(1)} async-done(((bf16[16,64,768]{2,1,0:T(8,128)(2,1)}), bf16[16,64,768]{2,1,0:T(8,128)(2,1)S(1)}, u32[]{:S(2)}, u32[]{:S(2)}) %all-to-all-start.5) | async-done | bytes 1572896 | tf_op jit(solution)/shard_map/all_to_all | solution.py:367
  146.6 1.0 multiply_reduce_fusion
  (36 shorter events, 5.5 us)
Async XLA Ops:
  0.6 12.3 %collective-permute-start = (bf16[128,768]{1,0:T(8,128)(2,1)}, bf16[128,768]{1,0:T(8,128)(2,1)}, u32[]{:S(2)}, u32[]{:S(2)}) collective-permute-start(bf16[128,768]{1,0:T(8,128)(2,1)} %param.5), channel_id=1, source_target_pairs={{0,2},{2,4},{4,6},{6,8},{8,10},{10,12},{12,14},{14,0},{1,3},{3,5},... | collective-permute-start | bytes 589832 | tf_op jit(solution)/shard_map/ppermute | solution.py:313
  2.6 12.3 %collective-permute-start.3 = (bf16[128,768]{1,0:T(8,128)(2,1)}, bf16[128,768]{1,0:T(8,128)(2,1)S(1)}, u32[]{:S(2)}, u32[]{:S(2)}) collective-permute-start(bf16[128,768]{1,0:T(8,128)(2,1)} %param.5), channel_id=1, source_target_pairs={{0,14},{2,0},{4,2},{6,4},{8,6},{10,8},{12,10},{14,12},{1,15},{3,1}... | collective-permute-start | bytes 589832 | tf_op jit(solution)/shard_map/ppermute | solution.py:313
  2.7 0.9 copy-start
  5.0 7.2 %copy-start.3 = (s32[64]{0:T(128)S(1)}, s32[64]{0:T(128)}, u32[]{:S(2)}) copy-start(s32[64]{0:T(128)} %param.7) | copy-start | bytes 772
  5.0 7.2 %copy-start.2 = (s32[128]{0:T(128)S(1)}, s32[128]{0:T(128)}, u32[]{:S(2)}) copy-start(s32[128]{0:T(128)} %param.6) | copy-start | bytes 1540
  5.0 7.9 %copy-start.1 = (bf16[128,768]{1,0:T(8,128)(2,1)S(1)}, bf16[128,768]{1,0:T(8,128)(2,1)}, u32[]{:S(2)}) copy-start(bf16[128,768]{1,0:T(8,128)(2,1)} %param.5) | copy-start | bytes 589828
  5.0 30.6 %all-to-all-start = ((bf16[16,64,768]{2,1,0:T(8,128)(2,1)}), bf16[16,64,768]{2,1,0:T(8,128)(2,1)S(1)}, u32[]{:S(2)}, u32[]{:S(2)}) async-start(bf16[16,64,768]{2,1,0:T(8,128)(2,1)} %shard_map.67), calls=%async_computation | async-start | bytes 3145728 | tf_op jit(solution)/shard_map/all_to_all | solution.py:321
  12.9 8.7 %collective-permute-start.1 = (bf16[128,768]{1,0:T(8,128)(2,1)}, bf16[128,768]{1,0:T(8,128)(2,1)S(1)}, u32[]{:S(2)}, u32[]{:S(2)}) collective-permute-start(bf16[128,768]{1,0:T(8,128)(2,1)} %collective-permute-done), channel_id=1, source_target_pairs={{0,2},{2,4},{4,6},{6,8},{8,10},{10,12},{12,14},{14,0},{1,3},{3,5},... | collective-permute-start | bytes 589832 | tf_op jit(solution)/shard_map/ppermute | solution.py:313
  14.9 7.1 %collective-permute-start.4 = (bf16[128,768]{1,0:T(8,128)(2,1)S(1)}, bf16[128,768]{1,0:T(8,128)(2,1)S(1)}, u32[]{:S(2)}, u32[]{:S(2)}) collective-permute-start(bf16[128,768]{1,0:T(8,128)(2,1)S(1)} %collective-permute-done.3), channel_id=1, source_target_pairs={{0,14},{2,0},{4,2},{6,4},{8,6},{10,8},{12,10},{14,12},{1,15},{3,1}... | collective-permute-start | bytes 589832 | tf_op jit(solution)/shard_map/ppermute | solution.py:313
  21.6 6.6 %collective-permute-start.2 = (bf16[128,768]{1,0:T(8,128)(2,1)S(1)}, bf16[128,768]{1,0:T(8,128)(2,1)S(1)}, u32[]{:S(2)}, u32[]{:S(2)}) collective-permute-start(bf16[128,768]{1,0:T(8,128)(2,1)S(1)} %collective-permute-done.1), channel_id=1, source_target_pairs={{0,2},{2,4},{4,6},{6,8},{8,10},{10,12},{12,14},{14,0},{1,3},{3,5},... | collective-permute-start | bytes 589832 | tf_op jit(solution)/shard_map/ppermute | solution.py:313
  22.0 6.6 %collective-permute-start.5 = (bf16[128,768]{1,0:T(8,128)(2,1)S(1)}, bf16[128,768]{1,0:T(8,128)(2,1)S(1)}, u32[]{:S(2)}, u32[]{:S(2)}) collective-permute-start(bf16[128,768]{1,0:T(8,128)(2,1)S(1)} %collective-permute-done.4), channel_id=1, source_target_pairs={{0,14},{2,0},{4,2},{6,4},{8,6},{10,8},{12,10},{14,12},{1,15},{3,1}... | collective-permute-start | bytes 589832 | tf_op jit(solution)/shard_map/ppermute | solution.py:313
  28.2 5.9 %collective-permute-start.6 = (bf16[64,768]{1,0:T(8,128)(2,1)S(1)}, bf16[64,768]{1,0:T(8,128)(2,1)S(1)}, u32[]{:S(2)}, u32[]{:S(2)}) collective-permute-start(bf16[64,768]{1,0:T(8,128)(2,1)S(1)} %slice.12), channel_id=1, source_target_pairs={{0,2},{2,4},{4,6},{6,8},{8,10},{10,12},{12,14},{14,0},{1,3},{3,5},... | collective-permute-start | bytes 294920 | tf_op jit(solution)/shard_map/ppermute | solution.py:313
  28.6 6.1 %collective-permute-start.7 = (bf16[64,768]{1,0:T(8,128)(2,1)S(1)}, bf16[64,768]{1,0:T(8,128)(2,1)S(1)}, u32[]{:S(2)}, u32[]{:S(2)}) collective-permute-start(bf16[64,768]{1,0:T(8,128)(2,1)S(1)} %slice.13), channel_id=1, source_target_pairs={{0,14},{2,0},{4,2},{6,4},{8,6},{10,8},{12,10},{14,12},{1,15},{3,1}... | collective-permute-start | bytes 294920 | tf_op jit(solution)/shard_map/ppermute | solution.py:313
  35.6 3.4 %collective-permute-start.8 = (bf16[1024,768]{1,0:T(8,128)(2,1)S(1)}, bf16[1024,768]{1,0:T(8,128)(2,1)S(1)}, u32[]{:S(2)}, u32[]{:S(2)}) collective-permute-start(bf16[1024,768]{1,0:T(8,128)(2,1)S(1)} %constant_dynamic-update-slice_fusion.y_ref.ya_ref), channel_id=1, source_target_pairs={{0,16},{16,0},{1,17},{17,1},{2,18},{18,2},{3,19},{19,3},{4,20},{20... | collective-permute-start | bytes 4718600 | tf_op jit(solution)/shard_map/ppermute | solution.py:337
  121.0 25.5 %all-to-all-start.5 = ((bf16[16,64,768]{2,1,0:T(8,128)(2,1)}), bf16[16,64,768]{2,1,0:T(8,128)(2,1)S(1)}, u32[]{:S(2)}, u32[]{:S(2)}) async-start(bf16[16,64,768]{2,1,0:T(8,128)(2,1)} %bitcast.11), calls=%async_computation.5 | async-start | bytes 3145728 | tf_op jit(solution)/shard_map/all_to_all | solution.py:367
  125.4 3.6 %collective-permute-start.9 = (f32[8,128]{1,0:T(8,128)S(1)}, f32[8,128]{1,0:T(8,128)S(1)}, u32[]{:S(2)}, u32[]{:S(2)}) collective-permute-start(f32[8,128]{1,0:T(8,128)S(1)} %get-tuple-element.33), channel_id=1, source_target_pairs={{0,2},{2,0},{4,6},{6,4},{8,10},{10,8},{12,14},{14,12},{1,3},{3,1},... | collective-permute-start | bytes 12296 | tf_op jit(solution)/shard_map/ppermute | solution.py:375
  129.0 4.5 %collective-permute-start.10 = (f32[8,128]{1,0:T(8,128)S(1)}, f32[8,128]{1,0:T(8,128)S(1)}, u32[]{:S(2)}, u32[]{:S(2)}) collective-permute-start(f32[8,128]{1,0:T(8,128)S(1)} %add.28), channel_id=1, source_target_pairs={{0,4},{2,6},{4,0},{6,2},{8,12},{10,14},{12,8},{14,10},{1,5},{3,7},... | collective-permute-start | bytes 12296 | tf_op jit(solution)/shard_map/ppermute | solution.py:375
  133.5 7.5 %collective-permute-start.11 = (f32[8,128]{1,0:T(8,128)S(1)}, f32[8,128]{1,0:T(8,128)S(1)}, u32[]{:S(2)}, u32[]{:S(2)}) collective-permute-start(f32[8,128]{1,0:T(8,128)S(1)} %add.29), channel_id=1, source_target_pairs={{0,8},{2,10},{4,12},{6,14},{8,0},{10,2},{12,4},{14,6},{1,9},{3,11}... | collective-permute-start | bytes 12296 | tf_op jit(solution)/shard_map/ppermute | solution.py:375

commit v2 on v1

--- a/solution.py
+++ b/solution.py
@@ -16,7 +16,7 @@
 COL = ("z", "xh")
 CG = ("xh", "xl", "y")
 TG = ("core", "z")
-RING = (0, -1, -2, -3, 1, 2, 3, 4)
+RING = (0, -1, 1, -2, 2, -3, 3, 4)
 LANE = 128
 SUB = 64
 BLK = 256
@@ -203,7 +203,7 @@
         copies(out_ref, k, fold_lanes(m_ref[here, :], l_ref[here, :]))
 
 
-def plan_kernel(parts_ref, logb_ref, ca_ref, cb_ref, ya_ref, yb_ref, out_ref, p_ref, v_ref, pot_ref, plan_ref, held_ref, sems):
+def plan_kernel(parts_ref, logb_ref, ca_ref, cb_ref, ya_ref, yb_ref, out_ref, p_ref, v_ref, pot_ref, held_ref, sems):
     rows, half = ca_ref.shape
     tgt_pot(parts_ref[...], logb_ref, v_ref, pot_ref)
     first = 2 * rows // LANE
@@ -214,32 +214,33 @@
         copies(out_ref, k, jnp.zeros((1, LANE), jnp.float32))
 
     leaving = []
-    for k in range(rows // LANE):
-        here = pl.ds(k * LANE, LANE)
-        score, tiles = scores(v_ref, ca_ref, cb_ref, here)
-        m = score(0)
-        for t in range(1, tiles):
-            m = jnp.maximum(m, score(t))
-        m = jnp.broadcast_to(jnp.max(m, axis=1, keepdims=True), (LANE, LANE))
-        l = jnp.zeros((LANE, LANE), jnp.float32)
-        for t in range(tiles):
-            p = jnp.exp2(score(t) - m)
-            l = l + p
-            plan_ref[here, pl.ds(t * LANE, LANE)] = p.astype(jnp.bfloat16)
-        m = m.T[:1, :]
-        l = jnp.sum(l.T, axis=0, keepdims=True)
-        copies(out_ref, k, m + jnp.log2(l))
-        copies(out_ref, rows // LANE + k, m)
-        if (k + 1) * LANE % BLK == 0:
-            here = pl.ds((k + 1) * LANE - BLK, BLK)
-            total = jnp.dot(plan_ref[here, pl.ds(0, half)], ya_ref[...], preferred_element_type=jnp.float32)
-            total = total + jnp.dot(
-                plan_ref[here, pl.ds(half, half)], yb_ref[...], preferred_element_type=jnp.float32
-            )
-            held_ref[here, :] = total.astype(jnp.bfloat16)
-            copy = pltpu.make_async_copy(held_ref.at[here], p_ref.at[here], sems.at[k * LANE // BLK])
-            copy.start()
-            leaving.append(copy)
+    for b in range(0, rows, BLK):
+        plan = []
+        for k in range(b // LANE, (b + BLK) // LANE):
+            score, tiles = scores(v_ref, ca_ref, cb_ref, pl.ds(k * LANE, LANE))
+            m = score(0)
+            for t in range(1, tiles):
+                m = jnp.maximum(m, score(t))
+            m = jnp.broadcast_to(jnp.max(m, axis=1, keepdims=True), (LANE, LANE))
+            l = jnp.zeros((LANE, LANE), jnp.float32)
+            row = []
+            for t in range(tiles):
+                p = jnp.exp2(score(t) - m)
+                l = l + p
+                row.append(p.astype(jnp.bfloat16))
+            plan.append(jnp.concatenate(row, axis=1))
+            m = m.T[:1, :]
+            l = jnp.sum(l.T, axis=0, keepdims=True)
+            copies(out_ref, k, m + jnp.log2(l))
+            copies(out_ref, rows // LANE + k, m)
+        plan = jnp.concatenate(plan, axis=0)
+        total = jnp.dot(plan[:, :half], ya_ref[...], preferred_element_type=jnp.float32)
+        total = total + jnp.dot(plan[:, half:], yb_ref[...], preferred_element_type=jnp.float32)
+        here = pl.ds(b, BLK)
+        held_ref[here, :] = total.astype(jnp.bfloat16)
+        copy = pltpu.make_async_copy(held_ref.at[here], p_ref.at[here], sems.at[b // BLK])
+        copy.start()
+        leaving.append(copy)
     for copy in leaving:
         copy.wait()
 
@@ -297,7 +298,7 @@
     total_rows = rows * pairs
     total_cols = cols * plane
 
-    def run(kernel, args, outs, scratch=(), special=()):
+    def run(kernel, args, outs, scratch=(), special=(), cost=rows * cols):
         special = dict(special)
         return pl.pallas_call(
             kernel,
@@ -306,7 +307,7 @@
             out_shape=[(pltpu.HBM if len(o) > 2 else jax.ShapeDtypeStruct)(o[0], o[1]) for o in outs],
             scratch_shapes=[pltpu.VMEM(*v) if isinstance(v, tuple) else v for v in scratch],
             compiler_params=pltpu.CompilerParams(vmem_limit_bytes=VMEM_LIMIT),
-            cost_estimate=pl.CostEstimate(flops=rows * cols * width, bytes_accessed=4 * rows * cols, transcendentals=rows * cols),
+            cost_estimate=pl.CostEstimate(flops=cost * width, bytes_accessed=4 * cost, transcendentals=cost),
         )(*[pltpu.with_memory_space_constraint(a, pltpu.HBM) if special.get(i) is HBM else a for i, a in enumerate(args)])
 
     def shift(block, by):
@@ -317,21 +318,22 @@
         (candidates,),
         [((plane, share, width), bf16, HBM)],
         [pltpu.SemaphoreType.DMA((plane,))],
-    )
+        cost=1,
+    )
+    x, targets = lax.optimization_barrier((x, targets))
     x = lax.all_to_all(x, CG, 0, 0, tiled=True).reshape(rows, width)
-    up, down = [targets], [targets]
-    for _ in range(depth // 2 - 1):
-        up.append(shift(up[-1], 1))
-        down.append(shift(down[-1], -1))
-    mid = targets.shape[0] // 2
-    ends = [shift(up[-1][:mid], 1), shift(down[-1][mid:], -1)]
-    ya = jnp.concatenate(up + down[1:] + ends, axis=0)
     counts = domain_counts.astype(f32)
     domains = jnp.arange(domain_counts.shape[0], dtype=jnp.int32)
     weight = jnp.sum(jnp.where(target_domain[:, None] == domains[None, :], counts[None, :], 0.0), axis=1)
     logb = jnp.log2(weight / jnp.sum(counts)) + (
         math.log2(domain_counts.shape[0]) - math.log2(total_cols)
     )
+    mid = targets.shape[0] // 2
+    late, logb = lax.optimization_barrier((targets, logb))
+    near = [shift(late, 1), shift(late, -1), shift(targets, 2), shift(targets, -2)]
+    far = [shift(near[2], 1), shift(near[3], -1)]
+    ends = [shift(far[0][:mid], 1), shift(far[1][mid:], -1)]
+    ya = jnp.concatenate([targets] + near + far + ends, axis=0)
     scale = TO2 / width
     ya, x, logb = lax.optimization_barrier((ya, x, logb[None, :]))
     yb = lax.ppermute(ya, "core", [(0, 1), (1, 0)])
@@ -361,7 +363,7 @@
         plan_kernel,
         (columns(out, col_shape), logb, ca, cb, ya, yb),
         [last_shape, ((rows, width), bf16, HBM)],
-        [vec, vec, ((rows, cols), bf16), ((rows, width), bf16), pltpu.SemaphoreType.DMA((rows // BLK,))],
+        [vec, vec, ((rows, width), bf16), pltpu.SemaphoreType.DMA((rows // BLK,))],
     )
     parts = lax.all_to_all(out, CG, 0, 0, tiled=True)
     moved = lax.all_to_all(partial.reshape(plane, share, width), CG, 0, 0, tiled=True)

time: 148 us -> 147 us (level)
  blocking collectives: 65.8 us -> 62 us
  waiting for transfers between devices: 29.5 us -> 32.6 us
    all_to_all x2, blocking collectives: 24.7 us -> 22.2 us  [columns(): parts = lax.all_to_all(out, CG, 0, 0, tiled=True)]
    all_to_all x1, waiting for transfers between devices: 0.81 us -> 3.23 us  [local(): x = lax.all_to_all(x, CG, 0, 0, tiled=True).reshape(rows, width)]
  transfers between devices with their start and end apart: 14 -> 14, of which waited for: 12 -> 10; matrix products, arithmetic and copies ran while one was open for 2% -> 2% of each run, Pallas kernels for 3% -> 2%
where the time goes in v2:
time: 147 us
  blocking collectives  62 us (42%)
  waiting for transfers between devices  32.6 us (22%)
  starting transfers between devices  26.1 us (18%)
  Pallas kernels  20.4 us (14%)
  other arithmetic  2.96 us (2%)
  local copies, waits for them, and re-layouts  1.96 us (1%)
    all_to_all x2, blocking collectives, columns(): return lax.all_to_all(out, TG, 0, 0, tiled=True)  28.5 us
    all_to_all x2, blocking collectives, columns(): parts = lax.all_to_all(out, CG, 0, 0, tiled=True)  22.2 us
    pallas_call x8, Pallas kernels, run(): pl.pallas_call(kernel, in_specs=[special.get(i, VMEM) for i in range(len(...  20.4 us
    ppermute x3, waiting for transfers between devices, local(): cand = cand + lax.ppermute(cand, 'z', [(i, i ^ bit) for i in range(depth)])  12.9 us
    ppermute x8, starting transfers between devices, shift(): lax.ppermute(block, 'z', [(i, (i + by) % depth) for i in range(depth)])  12.6 us
    all_to_all x1, blocking collectives, local(): parts = lax.all_to_all(out, CG, 0, 0, tiled=True)  11.3 us
    ppermute x8, waiting for transfers between devices, shift(): lax.ppermute(block, 'z', [(i, (i + by) % depth) for i in range(depth)])  10.7 us
    all_to_all x1, starting transfers between devices, local(): x = lax.all_to_all(x, CG, 0, 0, tiled=True).reshape(rows, width)  7.03 us
  transfers between devices with their start and end apart: 14, of which 10 were waited for; matrix products, arithmetic and copies ran while one was open for 2% of the time, Pallas kernels for 2%

profile of v2, /device:TPU:32, one launch (start us, length us, event | category | flops | bytes accessed | tf_op | source)
XLA Modules:
  0.0 146.8 jit_solution(3111730635073617761)
XLA Ops:
  1.5 1.3 shard_map.67
  2.9 5.5 %collective-permute-start.3 = (bf16[128,768]{1,0:T(8,128)(2,1)S(1)}, bf16[128,768]{1,0:T(8,128)(2,1)}, u32[]{:S(2)}, u32[]{:S(2)}) collective-permute-start(bf16[128,768]{1,0:T(8,128)(2,1)S(1)} %copy-done.1), channel_id=1, source_target_pairs={{0,12},{2,14},{4,0},{6,2},{8,4},{10,6},{12,8},{14,10},{1,13},{3,15... | collective-permute-start | bytes 589832 | tf_op jit(solution)/shard_map/ppermute | solution.py:314
  8.4 7.0 %all-to-all-start = ((bf16[16,64,768]{2,1,0:T(8,128)(2,1)}), bf16[16,64,768]{2,1,0:T(8,128)(2,1)S(1)}, u32[]{:S(2)}, u32[]{:S(2)}) async-start(bf16[16,64,768]{2,1,0:T(8,128)(2,1)} %shard_map.67), calls=%async_computation | async-start | bytes 3145728 | tf_op jit(solution)/shard_map/all_to_all | solution.py:324
  16.8 1.2 collective-permute-start
  17.9 0.9 collective-permute-start.1
  18.9 2.8 %collective-permute-start.5 = (bf16[128,768]{1,0:T(8,128)(2,1)}, bf16[128,768]{1,0:T(8,128)(2,1)S(1)}, u32[]{:S(2)}, u32[]{:S(2)}) collective-permute-start(bf16[128,768]{1,0:T(8,128)(2,1)} %collective-permute-done.3), channel_id=1, source_target_pairs={{0,14},{2,0},{4,2},{6,4},{8,6},{10,8},{12,10},{14,12},{1,15},{3,1}... | collective-permute-start | bytes 589832 | tf_op jit(solution)/shard_map/ppermute | solution.py:314
  21.8 3.4 %collective-permute-done = bf16[128,768]{1,0:T(8,128)(2,1)S(1)} collective-permute-done((bf16[128,768]{1,0:T(8,128)(2,1)S(1)}, bf16[128,768]{1,0:T(8,128)(2,1)S(1)}, u32[]{:S(2)}, u32[]{:S(2)}) %collective-permute-start) | collective-permute-done | bytes 196640 | tf_op jit(solution)/shard_map/ppermute | solution.py:314
  25.8 0.9 constant_dynamic-update-slice_fusion.4
  26.8 1.2 collective-permute-done.5
  28.0 1.3 collective-permute-start.7
  30.2 5.4 %collective-permute-done.6 = bf16[64,768]{1,0:T(8,128)(2,1)S(1)} collective-permute-done((bf16[64,768]{1,0:T(8,128)(2,1)S(1)}, bf16[64,768]{1,0:T(8,128)(2,1)S(1)}, u32[]{:S(2)}, u32[]{:S(2)}) %collective-permute-start.6) | collective-permute-done | bytes 98336 | tf_op jit(solution)/shard_map/ppermute | solution.py:314
  35.7 3.2 %all-to-all-done = bf16[16,64,768]{2,1,0:T(8,128)(2,1)S(1)} async-done(((bf16[16,64,768]{2,1,0:T(8,128)(2,1)}), bf16[16,64,768]{2,1,0:T(8,128)(2,1)S(1)}, u32[]{:S(2)}, u32[]{:S(2)}) %all-to-all-start) | async-done | bytes 1572896 | tf_op jit(solution)/shard_map/all_to_all | solution.py:324
  38.9 2.5 %shard_map.68 = (f32[1024,1024]{1,0:T(8,128)S(1)}, f32[1024,128]{1,0:T(8,128)S(1)}, f32[1024,128]{1,0:T(8,128)S(1)}, f32[1024,128]{1,0:T(8,128)S(1)}) custom-call(bf16[1024,768]{1,0:T(8,128)(2,1)S(1)} %bitcast.7, bf16[1024,768]{1,0:T(8,128)(2,1)S(1)} %constant_dynamic-update-slice_fusion.y_ref.ya_ref), custom_call_target="tpu_custom_call" | custom-call | flops 1610612736 | bytes 8388608 | tf_op jit(solution)/shard_map/pallas_call | solution.py:303
  41.4 0.9 collective-permute-done.8.y_ref.yb_ref
  42.3 2.5 %shard_map.69 = (f32[1024,1024]{1,0:T(8,128)S(1)}, f32[16,8,128]{2,1,0:T(8,128)S(1)}) custom-call(bf16[1024,768]{1,0:T(8,128)(2,1)S(1)} %bitcast.8, f32[1024,128]{1,0:T(8,128)S(1)} %get-tuple-element.29.sqx_ref, bf16[1024,768]{1,0:T(8,128)(2,1)S(1)} %collective-permute-done.8.y_ref.yb_ref, f32[1024,128]{1,0:T(8,128)S(1)} %get-tuple-element.30.m0_ref, ...), custom_call_target="tpu_custom_call" | custom-call | flops 1610612736 | bytes 8388608 | tf_op jit(solution)/shard_map/pallas_call | solution.py:303
  44.9 11.3 %all_to_all.35.parts_ref = f32[16,8,128]{2,1,0:T(8,128)S(1)} all-to-all(f32[16,8,128]{2,1,0:T(8,128)S(1)} %get-tuple-element.32), channel_id=1, replica_groups=mesh['xl'=2,'y'=4,'core'=2,'z'=8,'xh'=2] {'xh','xl','y'}, dimensions={0} | all-to-all | bytes 131072 | tf_op jit(solution)/shard_map/all_to_all | solution.py:355
  56.1 2.7 %shard_map.70 = f32[16,24,128]{2,1,0:T(8,128)S(1)} custom-call(f32[16,8,128]{2,1,0:T(8,128)S(1)} %all_to_all.35.parts_ref, f32[1024,1024]{1,0:T(8,128)S(1)} %get-tuple-element.33.ca_ref, f32[1024,1024]{1,0:T(8,128)S(1)} %get-tuple-element.34.cb_ref, f32[1,128]{1,0:T(1,128)S(1)} %bitcast.10), custom_call_target="tpu_custom_call" | custom-call | flops 1610612736 | bytes 8388608 | tf_op jit(solution)/shard_map/pallas_call | solution.py:303
  58.8 16.9 %all_to_all.36.parts_ref = f32[16,24,128]{2,1,0:T(8,128)S(1)} all-to-all(f32[16,24,128]{2,1,0:T(8,128)S(1)} %shard_map.70), channel_id=1, replica_groups=mesh['xl'=2,'y'=4,'core'=2,'z'=8,'xh'=2] {'core','z'}, dimensions={0} | all-to-all | bytes 393216 | tf_op jit(solution)/shard_map/all_to_all | solution.py:357
  75.8 2.4 %shard_map.71 = (f32[16,8,128]{2,1,0:T(8,128)S(1)}, f32[16,128]{1,0:T(8,128)S(1)}) custom-call(f32[16,24,128]{2,1,0:T(8,128)S(1)} %all_to_all.36.parts_ref, f32[1024,1024]{1,0:T(8,128)S(1)} %get-tuple-element.33.ca_ref, f32[1024,1024]{1,0:T(8,128)S(1)} %get-tuple-element.34.cb_ref), custom_call_target="tpu_custom_call" | custom-call | flops 1610612736 | bytes 8388608 | tf_op jit(solution)/shard_map/pallas_call | solution.py:303
  78.1 10.9 %all_to_all.37.parts_ref = f32[16,8,128]{2,1,0:T(8,128)S(1)} all-to-all(f32[16,8,128]{2,1,0:T(8,128)S(1)} %get-tuple-element.36), channel_id=1, replica_groups=mesh['xl'=2,'y'=4,'core'=2,'z'=8,'xh'=2] {'xh','xl','y'}, dimensions={0} | all-to-all | bytes 131072 | tf_op jit(solution)/shard_map/all_to_all | solution.py:355
  89.0 2.7 %shard_map.72 = f32[16,16,128]{2,1,0:T(8,128)S(1)} custom-call(f32[16,8,128]{2,1,0:T(8,128)S(1)} %all_to_all.37.parts_ref, f32[1024,1024]{1,0:T(8,128)S(1)} %get-tuple-element.33.ca_ref, f32[1024,1024]{1,0:T(8,128)S(1)} %get-tuple-element.34.cb_ref), custom_call_target="tpu_custom_call" | custom-call | flops 1610612736 | bytes 8388608 | tf_op jit(solution)/shard_map/pallas_call | solution.py:303
  91.7 11.6 %all_to_all.38.parts_ref = f32[16,16,128]{2,1,0:T(8,128)S(1)} all-to-all(f32[16,16,128]{2,1,0:T(8,128)S(1)} %shard_map.72), channel_id=1, replica_groups=mesh['xl'=2,'y'=4,'core'=2,'z'=8,'xh'=2] {'core','z'}, dimensions={0} | all-to-all | bytes 262144 | tf_op jit(solution)/shard_map/all_to_all | solution.py:357
  103.3 5.7 %shard_map.73 = (f32[16,24,128]{2,1,0:T(8,128)S(1)}, bf16[1024,768]{1,0:T(8,128)(2,1)}) custom-call(f32[16,16,128]{2,1,0:T(8,128)S(1)} %all_to_all.38.parts_ref, f32[16,128]{1,0:T(8,128)S(1)} %get-tuple-element.37.logb_ref, f32[1024,1024]{1,0:T(8,128)S(1)} %get-tuple-element.33.ca_ref, f32[1024,1024]{1,0:T(8,128)S(1)} %get-tuple-element.34.cb_ref, ...), custom_call_target="tpu_custom_call" | custom-call | flops 1610612736 | bytes 8388608 | tf_op jit(solution)/shard_map/pallas_call | solution.py:303
  109.0 11.3 %all_to_all.39.parts_ref = f32[16,24,128]{2,1,0:T(8,128)S(1)} all-to-all(f32[16,24,128]{2,1,0:T(8,128)S(1)} %get-tuple-element.39), channel_id=1, replica_groups=mesh['xl'=2,'y'=4,'core'=2,'z'=8,'xh'=2] {'xh','xl','y'}, dimensions={0} | all-to-all | bytes 393216 | tf_op jit(solution)/shard_map/all_to_all | solution.py:368
  120.3 3.7 %all-to-all-start.5 = ((bf16[16,64,768]{2,1,0:T(8,128)(2,1)}), bf16[16,64,768]{2,1,0:T(8,128)(2,1)S(1)}, u32[]{:S(2)}, u32[]{:S(2)}) async-start(bf16[16,64,768]{2,1,0:T(8,128)(2,1)} %bitcast.11), calls=%async_computation.5 | async-start | bytes 3145728 | tf_op jit(solution)/shard_map/all_to_all | solution.py:369
  125.0 3.2 %collective-permute-done.9 = f32[8,128]{1,0:T(8,128)S(1)} collective-permute-done((f32[8,128]{1,0:T(8,128)S(1)}, f32[8,128]{1,0:T(8,128)S(1)}, u32[]{:S(2)}, u32[]{:S(2)}) %collective-permute-start.9) | collective-permute-done | bytes 4128 | tf_op jit(solution)/shard_map/ppermute | solution.py:377
  128.3 0.9 collective-permute-start.10
  129.2 3.6 %collective-permute-done.10 = f32[8,128]{1,0:T(8,128)S(1)} collective-permute-done((f32[8,128]{1,0:T(8,128)S(1)}, f32[8,128]{1,0:T(8,128)S(1)}, u32[]{:S(2)}, u32[]{:S(2)}) %collective-permute-start.10) | collective-permute-done | bytes 4128 | tf_op jit(solution)/shard_map/ppermute | solution.py:377
  132.8 1.5 %collective-permute-start.11 = (f32[8,128]{1,0:T(8,128)S(1)}, f32[8,128]{1,0:T(8,128)S(1)}, u32[]{:S(2)}, u32[]{:S(2)}) collective-permute-start(f32[8,128]{1,0:T(8,128)S(1)} %add.18), channel_id=1, source_target_pairs={{0,8},{2,10},{4,12},{6,14},{8,0},{10,2},{12,4},{14,6},{1,9},{3,11}... | collective-permute-start | bytes 12296 | tf_op jit(solution)/shard_map/ppermute | solution.py:377
  134.3 6.0 %collective-permute-done.11 = f32[8,128]{1,0:T(8,128)S(1)} collective-permute-done((f32[8,128]{1,0:T(8,128)S(1)}, f32[8,128]{1,0:T(8,128)S(1)}, u32[]{:S(2)}, u32[]{:S(2)}) %collective-permute-start.11) | collective-permute-done | bytes 4128 | tf_op jit(solution)/shard_map/ppermute | solution.py:377
  140.9 4.9 %all-to-all-done.5 = bf16[16,64,768]{2,1,0:T(8,128)(2,1)S(1)} async-done(((bf16[16,64,768]{2,1,0:T(8,128)(2,1)}), bf16[16,64,768]{2,1,0:T(8,128)(2,1)S(1)}, u32[]{:S(2)}, u32[]{:S(2)}) %all-to-all-start.5) | async-done | bytes 1572896 | tf_op jit(solution)/shard_map/all_to_all | solution.py:369
  145.8 1.0 multiply_reduce_fusion
  (36 shorter events, 5.5 us)
Async XLA Ops:
  0.6 0.9 copy-start
  1.5 1.3 copy-start.1
  2.9 12.6 %copy-start.2 = (s32[64]{0:T(128)S(1)}, s32[64]{0:T(128)}, u32[]{:S(2)}) copy-start(s32[64]{0:T(128)} %param.7) | copy-start | bytes 772
  2.9 13.2 %copy-start.3 = (s32[128]{0:T(128)S(1)}, s32[128]{0:T(128)}, u32[]{:S(2)}) copy-start(s32[128]{0:T(128)} %param.6) | copy-start | bytes 1540
  2.9 16.0 %collective-permute-start.3 = (bf16[128,768]{1,0:T(8,128)(2,1)S(1)}, bf16[128,768]{1,0:T(8,128)(2,1)}, u32[]{:S(2)}, u32[]{:S(2)}) collective-permute-start(bf16[128,768]{1,0:T(8,128)(2,1)S(1)} %copy-done.1), channel_id=1, source_target_pairs={{0,12},{2,14},{4,0},{6,2},{8,4},{10,6},{12,8},{14,10},{1,13},{3,15... | collective-permute-start | bytes 589832 | tf_op jit(solution)/shard_map/ppermute | solution.py:314
  8.4 13.4 %collective-permute-start.2 = (bf16[128,768]{1,0:T(8,128)(2,1)S(1)}, bf16[128,768]{1,0:T(8,128)(2,1)S(1)}, u32[]{:S(2)}, u32[]{:S(2)}) collective-permute-start(bf16[128,768]{1,0:T(8,128)(2,1)S(1)} %copy-done.1), channel_id=1, source_target_pairs={{0,4},{2,6},{4,8},{6,10},{8,12},{10,14},{12,0},{14,2},{1,5},{3,7},... | collective-permute-start | bytes 589832 | tf_op jit(solution)/shard_map/ppermute | solution.py:314
  8.4 30.5 %all-to-all-start = ((bf16[16,64,768]{2,1,0:T(8,128)(2,1)}), bf16[16,64,768]{2,1,0:T(8,128)(2,1)S(1)}, u32[]{:S(2)}, u32[]{:S(2)}) async-start(bf16[16,64,768]{2,1,0:T(8,128)(2,1)} %shard_map.67), calls=%async_computation | async-start | bytes 3145728 | tf_op jit(solution)/shard_map/all_to_all | solution.py:324
  16.8 8.4 %collective-permute-start = (bf16[128,768]{1,0:T(8,128)(2,1)S(1)}, bf16[128,768]{1,0:T(8,128)(2,1)S(1)}, u32[]{:S(2)}, u32[]{:S(2)}) collective-permute-start(bf16[128,768]{1,0:T(8,128)(2,1)S(1)} %copy-done.1), channel_id=1, source_target_pairs={{0,2},{2,4},{4,6},{6,8},{8,10},{10,12},{12,14},{14,0},{1,3},{3,5},... | collective-permute-start | bytes 589832 | tf_op jit(solution)/shard_map/ppermute | solution.py:314
  17.9 7.8 %collective-permute-start.1 = (bf16[128,768]{1,0:T(8,128)(2,1)S(1)}, bf16[128,768]{1,0:T(8,128)(2,1)S(1)}, u32[]{:S(2)}, u32[]{:S(2)}) collective-permute-start(bf16[128,768]{1,0:T(8,128)(2,1)S(1)} %copy-done.1), channel_id=1, source_target_pairs={{0,14},{2,0},{4,2},{6,4},{8,6},{10,8},{12,10},{14,12},{1,15},{3,1}... | collective-permute-start | bytes 589832 | tf_op jit(solution)/shard_map/ppermute | solution.py:314
  18.9 9.0 %collective-permute-start.5 = (bf16[128,768]{1,0:T(8,128)(2,1)}, bf16[128,768]{1,0:T(8,128)(2,1)S(1)}, u32[]{:S(2)}, u32[]{:S(2)}) collective-permute-start(bf16[128,768]{1,0:T(8,128)(2,1)} %collective-permute-done.3), channel_id=1, source_target_pairs={{0,14},{2,0},{4,2},{6,4},{8,6},{10,8},{12,10},{14,12},{1,15},{3,1}... | collective-permute-start | bytes 589832 | tf_op jit(solution)/shard_map/ppermute | solution.py:314
  21.8 7.5 %collective-permute-start.4 = (bf16[128,768]{1,0:T(8,128)(2,1)S(1)}, bf16[128,768]{1,0:T(8,128)(2,1)S(1)}, u32[]{:S(2)}, u32[]{:S(2)}) collective-permute-start(bf16[128,768]{1,0:T(8,128)(2,1)S(1)} %collective-permute-done.2), channel_id=1, source_target_pairs={{0,2},{2,4},{4,6},{6,8},{8,10},{10,12},{12,14},{14,0},{1,3},{3,5},... | collective-permute-start | bytes 589832 | tf_op jit(solution)/shard_map/ppermute | solution.py:314
  28.0 7.7 %collective-permute-start.7 = (bf16[64,768]{1,0:T(8,128)(2,1)S(1)}, bf16[64,768]{1,0:T(8,128)(2,1)S(1)}, u32[]{:S(2)}, u32[]{:S(2)}) collective-permute-start(bf16[64,768]{1,0:T(8,128)(2,1)S(1)} %slice.13), channel_id=1, source_target_pairs={{0,14},{2,0},{4,2},{6,4},{8,6},{10,8},{12,10},{14,12},{1,15},{3,1}... | collective-permute-start | bytes 294920 | tf_op jit(solution)/shard_map/ppermute | solution.py:314
  29.3 6.3 %collective-permute-start.6 = (bf16[64,768]{1,0:T(8,128)(2,1)S(1)}, bf16[64,768]{1,0:T(8,128)(2,1)S(1)}, u32[]{:S(2)}, u32[]{:S(2)}) collective-permute-start(bf16[64,768]{1,0:T(8,128)(2,1)S(1)} %slice.12), channel_id=1, source_target_pairs={{0,2},{2,4},{4,6},{6,8},{8,10},{10,12},{12,14},{14,0},{1,3},{3,5},... | collective-permute-start | bytes 294920 | tf_op jit(solution)/shard_map/ppermute | solution.py:314
  38.9 3.4 %collective-permute-start.8 = (bf16[1024,768]{1,0:T(8,128)(2,1)S(1)}, bf16[1024,768]{1,0:T(8,128)(2,1)S(1)}, u32[]{:S(2)}, u32[]{:S(2)}) collective-permute-start(bf16[1024,768]{1,0:T(8,128)(2,1)S(1)} %constant_dynamic-update-slice_fusion.y_ref.ya_ref), channel_id=1, source_target_pairs={{0,16},{16,0},{1,17},{17,1},{2,18},{18,2},{3,19},{19,3},{4,20},{20... | collective-permute-start | bytes 4718600 | tf_op jit(solution)/shard_map/ppermute | solution.py:339
  120.3 25.5 %all-to-all-start.5 = ((bf16[16,64,768]{2,1,0:T(8,128)(2,1)}), bf16[16,64,768]{2,1,0:T(8,128)(2,1)S(1)}, u32[]{:S(2)}, u32[]{:S(2)}) async-start(bf16[16,64,768]{2,1,0:T(8,128)(2,1)} %bitcast.11), calls=%async_computation.5 | async-start | bytes 3145728 | tf_op jit(solution)/shard_map/all_to_all | solution.py:369
  124.7 3.6 %collective-permute-start.9 = (f32[8,128]{1,0:T(8,128)S(1)}, f32[8,128]{1,0:T(8,128)S(1)}, u32[]{:S(2)}, u32[]{:S(2)}) collective-permute-start(f32[8,128]{1,0:T(8,128)S(1)} %get-tuple-element.41), channel_id=1, source_target_pairs={{0,2},{2,0},{4,6},{6,4},{8,10},{10,8},{12,14},{14,12},{1,3},{3,1},... | collective-permute-start | bytes 12296 | tf_op jit(solution)/shard_map/ppermute | solution.py:377
  128.3 4.5 %collective-permute-start.10 = (f32[8,128]{1,0:T(8,128)S(1)}, f32[8,128]{1,0:T(8,128)S(1)}, u32[]{:S(2)}, u32[]{:S(2)}) collective-permute-start(f32[8,128]{1,0:T(8,128)S(1)} %add.17), channel_id=1, source_target_pairs={{0,4},{2,6},{4,0},{6,2},{8,12},{10,14},{12,8},{14,10},{1,5},{3,7},... | collective-permute-start | bytes 12296 | tf_op jit(solution)/shard_map/ppermute | solution.py:377
  132.8 7.5 %collective-permute-start.11 = (f32[8,128]{1,0:T(8,128)S(1)}, f32[8,128]{1,0:T(8,128)S(1)}, u32[]{:S(2)}, u32[]{:S(2)}) collective-permute-start(f32[8,128]{1,0:T(8,128)S(1)} %add.18), channel_id=1, source_target_pairs={{0,8},{2,10},{4,12},{6,14},{8,0},{10,2},{12,4},{14,6},{1,9},{3,11}... | collective-permute-start | bytes 12296 | tf_op jit(solution)/shard_map/ppermute | solution.py:377

commit v3 on v2

--- a/solution.py
+++ b/solution.py
@@ -134,7 +134,7 @@
     u = log2a - merge(parts_ref[...])
     for k in range(rows // LANE):
         u_ref[pl.ds(k * LANE, LANE), :] = spread(u[k : k + 1, :])
-    sub, group = 32, 4
+    sub, group = 32, 8
     for h, c_ref in enumerate((ca_ref, cb_ref)):
         for k0 in range(0, half // LANE, group):
             ks = range(k0, k0 + group)

time: 147 us -> 147 us (level)
  no operation moved by 1% of the time
where the time goes in v3:
time: 147 us; the launch traced here: 146 us
  blocking collectives  62 us (42%)
  waiting for transfers between devices  32.6 us (22%)
  starting transfers between devices  26.1 us (18%)
  Pallas kernels  20 us (14%)
  other arithmetic  2.96 us (2%)
  local copies, waits for them, and re-layouts  1.96 us (1%)
    all_to_all x2, blocking collectives, columns(): return lax.all_to_all(out, TG, 0, 0, tiled=True)  28.5 us
    all_to_all x2, blocking collectives, columns(): parts = lax.all_to_all(out, CG, 0, 0, tiled=True)  22.2 us
    pallas_call x8, Pallas kernels, run(): pl.pallas_call(kernel, in_specs=[special.get(i, VMEM) for i in range(len(...  20 us
    ppermute x3, waiting for transfers between devices, local(): cand = cand + lax.ppermute(cand, 'z', [(i, i ^ bit) for i in range(depth)])  12.9 us
    ppermute x8, starting transfers between devices, shift(): lax.ppermute(block, 'z', [(i, (i + by) % depth) for i in range(depth)])  12.6 us
    all_to_all x1, blocking collectives, local(): parts = lax.all_to_all(out, CG, 0, 0, tiled=True)  11.3 us
    ppermute x8, waiting for transfers between devices, shift(): lax.ppermute(block, 'z', [(i, (i + by) % depth) for i in range(depth)])  10.7 us
    all_to_all x1, starting transfers between devices, local(): x = lax.all_to_all(x, CG, 0, 0, tiled=True).reshape(rows, width)  7.03 us
  transfers between devices with their start and end apart: 14, of which 10 were waited for; matrix products, arithmetic and copies ran while one was open for 2% of the time, Pallas kernels for 2%

profile of v3, /device:TPU:32, one launch (start us, length us, event | category | flops | bytes accessed | tf_op | source)
XLA Modules:
  0.0 146.5 jit_solution(6810959677954887807)
XLA Ops:
  1.5 1.3 shard_map.67
  2.9 5.5 %collective-permute-start.3 = (bf16[128,768]{1,0:T(8,128)(2,1)S(1)}, bf16[128,768]{1,0:T(8,128)(2,1)}, u32[]{:S(2)}, u32[]{:S(2)}) collective-permute-start(bf16[128,768]{1,0:T(8,128)(2,1)S(1)} %copy-done.1), channel_id=1, source_target_pairs={{0,12},{2,14},{4,0},{6,2},{8,4},{10,6},{12,8},{14,10},{1,13},{3,15... | collective-permute-start | bytes 589832 | tf_op jit(solution)/shard_map/ppermute | solution.py:314
  8.4 7.0 %all-to-all-start = ((bf16[16,64,768]{2,1,0:T(8,128)(2,1)}), bf16[16,64,768]{2,1,0:T(8,128)(2,1)S(1)}, u32[]{:S(2)}, u32[]{:S(2)}) async-start(bf16[16,64,768]{2,1,0:T(8,128)(2,1)} %shard_map.67), calls=%async_computation | async-start | bytes 3145728 | tf_op jit(solution)/shard_map/all_to_all | solution.py:324
  16.8 1.2 collective-permute-start
  17.9 0.9 collective-permute-start.1
  18.9 2.8 %collective-permute-start.5 = (bf16[128,768]{1,0:T(8,128)(2,1)}, bf16[128,768]{1,0:T(8,128)(2,1)S(1)}, u32[]{:S(2)}, u32[]{:S(2)}) collective-permute-start(bf16[128,768]{1,0:T(8,128)(2,1)} %collective-permute-done.3), channel_id=1, source_target_pairs={{0,14},{2,0},{4,2},{6,4},{8,6},{10,8},{12,10},{14,12},{1,15},{3,1}... | collective-permute-start | bytes 589832 | tf_op jit(solution)/shard_map/ppermute | solution.py:314
  21.8 3.4 %collective-permute-done = bf16[128,768]{1,0:T(8,128)(2,1)S(1)} collective-permute-done((bf16[128,768]{1,0:T(8,128)(2,1)S(1)}, bf16[128,768]{1,0:T(8,128)(2,1)S(1)}, u32[]{:S(2)}, u32[]{:S(2)}) %collective-permute-start) | collective-permute-done | bytes 196640 | tf_op jit(solution)/shard_map/ppermute | solution.py:314
  25.8 0.9 constant_dynamic-update-slice_fusion.4
  26.8 1.2 collective-permute-done.5
  28.0 1.3 collective-permute-start.7
  30.2 5.4 %collective-permute-done.6 = bf16[64,768]{1,0:T(8,128)(2,1)S(1)} collective-permute-done((bf16[64,768]{1,0:T(8,128)(2,1)S(1)}, bf16[64,768]{1,0:T(8,128)(2,1)S(1)}, u32[]{:S(2)}, u32[]{:S(2)}) %collective-permute-start.6) | collective-permute-done | bytes 98336 | tf_op jit(solution)/shard_map/ppermute | solution.py:314
  35.7 3.2 %all-to-all-done = bf16[16,64,768]{2,1,0:T(8,128)(2,1)S(1)} async-done(((bf16[16,64,768]{2,1,0:T(8,128)(2,1)}), bf16[16,64,768]{2,1,0:T(8,128)(2,1)S(1)}, u32[]{:S(2)}, u32[]{:S(2)}) %all-to-all-start) | async-done | bytes 1572896 | tf_op jit(solution)/shard_map/all_to_all | solution.py:324
  38.9 2.5 %shard_map.68 = (f32[1024,1024]{1,0:T(8,128)S(1)}, f32[1024,128]{1,0:T(8,128)S(1)}, f32[1024,128]{1,0:T(8,128)S(1)}, f32[1024,128]{1,0:T(8,128)S(1)}) custom-call(bf16[1024,768]{1,0:T(8,128)(2,1)S(1)} %bitcast.7, bf16[1024,768]{1,0:T(8,128)(2,1)S(1)} %constant_dynamic-update-slice_fusion.y_ref.ya_ref), custom_call_target="tpu_custom_call" | custom-call | flops 1610612736 | bytes 8388608 | tf_op jit(solution)/shard_map/pallas_call | solution.py:303
  41.4 0.9 collective-permute-done.8.y_ref.yb_ref
  42.3 2.5 %shard_map.69 = (f32[1024,1024]{1,0:T(8,128)S(1)}, f32[16,8,128]{2,1,0:T(8,128)S(1)}) custom-call(bf16[1024,768]{1,0:T(8,128)(2,1)S(1)} %bitcast.8, f32[1024,128]{1,0:T(8,128)S(1)} %get-tuple-element.29.sqx_ref, bf16[1024,768]{1,0:T(8,128)(2,1)S(1)} %collective-permute-done.8.y_ref.yb_ref, f32[1024,128]{1,0:T(8,128)S(1)} %get-tuple-element.30.m0_ref, ...), custom_call_target="tpu_custom_call" | custom-call | flops 1610612736 | bytes 8388608 | tf_op jit(solution)/shard_map/pallas_call | solution.py:303
  44.9 11.3 %all_to_all.35.parts_ref = f32[16,8,128]{2,1,0:T(8,128)S(1)} all-to-all(f32[16,8,128]{2,1,0:T(8,128)S(1)} %get-tuple-element.32), channel_id=1, replica_groups=mesh['xl'=2,'y'=4,'core'=2,'z'=8,'xh'=2] {'xh','xl','y'}, dimensions={0} | all-to-all | bytes 131072 | tf_op jit(solution)/shard_map/all_to_all | solution.py:355
  56.1 2.5 %shard_map.70 = f32[16,24,128]{2,1,0:T(8,128)S(1)} custom-call(f32[16,8,128]{2,1,0:T(8,128)S(1)} %all_to_all.35.parts_ref, f32[1024,1024]{1,0:T(8,128)S(1)} %get-tuple-element.33.ca_ref, f32[1024,1024]{1,0:T(8,128)S(1)} %get-tuple-element.34.cb_ref, f32[1,128]{1,0:T(1,128)S(1)} %bitcast.10), custom_call_target="tpu_custom_call" | custom-call | flops 1610612736 | bytes 8388608 | tf_op jit(solution)/shard_map/pallas_call | solution.py:303
  58.7 16.9 %all_to_all.36.parts_ref = f32[16,24,128]{2,1,0:T(8,128)S(1)} all-to-all(f32[16,24,128]{2,1,0:T(8,128)S(1)} %shard_map.70), channel_id=1, replica_groups=mesh['xl'=2,'y'=4,'core'=2,'z'=8,'xh'=2] {'core','z'}, dimensions={0} | all-to-all | bytes 393216 | tf_op jit(solution)/shard_map/all_to_all | solution.py:357
  75.6 2.4 %shard_map.71 = (f32[16,8,128]{2,1,0:T(8,128)S(1)}, f32[16,128]{1,0:T(8,128)S(1)}) custom-call(f32[16,24,128]{2,1,0:T(8,128)S(1)} %all_to_all.36.parts_ref, f32[1024,1024]{1,0:T(8,128)S(1)} %get-tuple-element.33.ca_ref, f32[1024,1024]{1,0:T(8,128)S(1)} %get-tuple-element.34.cb_ref), custom_call_target="tpu_custom_call" | custom-call | flops 1610612736 | bytes 8388608 | tf_op jit(solution)/shard_map/pallas_call | solution.py:303
  78.0 10.9 %all_to_all.37.parts_ref = f32[16,8,128]{2,1,0:T(8,128)S(1)} all-to-all(f32[16,8,128]{2,1,0:T(8,128)S(1)} %get-tuple-element.36), channel_id=1, replica_groups=mesh['xl'=2,'y'=4,'core'=2,'z'=8,'xh'=2] {'xh','xl','y'}, dimensions={0} | all-to-all | bytes 131072 | tf_op jit(solution)/shard_map/all_to_all | solution.py:355
  88.8 2.5 %shard_map.72 = f32[16,16,128]{2,1,0:T(8,128)S(1)} custom-call(f32[16,8,128]{2,1,0:T(8,128)S(1)} %all_to_all.37.parts_ref, f32[1024,1024]{1,0:T(8,128)S(1)} %get-tuple-element.33.ca_ref, f32[1024,1024]{1,0:T(8,128)S(1)} %get-tuple-element.34.cb_ref), custom_call_target="tpu_custom_call" | custom-call | flops 1610612736 | bytes 8388608 | tf_op jit(solution)/shard_map/pallas_call | solution.py:303
  91.4 11.6 %all_to_all.38.parts_ref = f32[16,16,128]{2,1,0:T(8,128)S(1)} all-to-all(f32[16,16,128]{2,1,0:T(8,128)S(1)} %shard_map.72), channel_id=1, replica_groups=mesh['xl'=2,'y'=4,'core'=2,'z'=8,'xh'=2] {'core','z'}, dimensions={0} | all-to-all | bytes 262144 | tf_op jit(solution)/shard_map/all_to_all | solution.py:357
  103.0 5.7 %shard_map.73 = (f32[16,24,128]{2,1,0:T(8,128)S(1)}, bf16[1024,768]{1,0:T(8,128)(2,1)}) custom-call(f32[16,16,128]{2,1,0:T(8,128)S(1)} %all_to_all.38.parts_ref, f32[16,128]{1,0:T(8,128)S(1)} %get-tuple-element.37.logb_ref, f32[1024,1024]{1,0:T(8,128)S(1)} %get-tuple-element.33.ca_ref, f32[1024,1024]{1,0:T(8,128)S(1)} %get-tuple-element.34.cb_ref, ...), custom_call_target="tpu_custom_call" | custom-call | flops 1610612736 | bytes 8388608 | tf_op jit(solution)/shard_map/pallas_call | solution.py:303
  108.6 11.3 %all_to_all.39.parts_ref = f32[16,24,128]{2,1,0:T(8,128)S(1)} all-to-all(f32[16,24,128]{2,1,0:T(8,128)S(1)} %get-tuple-element.39), channel_id=1, replica_groups=mesh['xl'=2,'y'=4,'core'=2,'z'=8,'xh'=2] {'xh','xl','y'}, dimensions={0} | all-to-all | bytes 393216 | tf_op jit(solution)/shard_map/all_to_all | solution.py:368
  119.9 3.7 %all-to-all-start.5 = ((bf16[16,64,768]{2,1,0:T(8,128)(2,1)}), bf16[16,64,768]{2,1,0:T(8,128)(2,1)S(1)}, u32[]{:S(2)}, u32[]{:S(2)}) async-start(bf16[16,64,768]{2,1,0:T(8,128)(2,1)} %bitcast.11), calls=%async_computation.5 | async-start | bytes 3145728 | tf_op jit(solution)/shard_map/all_to_all | solution.py:369
  124.7 3.3 %collective-permute-done.9 = f32[8,128]{1,0:T(8,128)S(1)} collective-permute-done((f32[8,128]{1,0:T(8,128)S(1)}, f32[8,128]{1,0:T(8,128)S(1)}, u32[]{:S(2)}, u32[]{:S(2)}) %collective-permute-start.9) | collective-permute-done | bytes 4128 | tf_op jit(solution)/shard_map/ppermute | solution.py:377
  127.9 0.9 collective-permute-start.10
  128.8 3.6 %collective-permute-done.10 = f32[8,128]{1,0:T(8,128)S(1)} collective-permute-done((f32[8,128]{1,0:T(8,128)S(1)}, f32[8,128]{1,0:T(8,128)S(1)}, u32[]{:S(2)}, u32[]{:S(2)}) %collective-permute-start.10) | collective-permute-done | bytes 4128 | tf_op jit(solution)/shard_map/ppermute | solution.py:377
  132.4 1.5 %collective-permute-start.11 = (f32[8,128]{1,0:T(8,128)S(1)}, f32[8,128]{1,0:T(8,128)S(1)}, u32[]{:S(2)}, u32[]{:S(2)}) collective-permute-start(f32[8,128]{1,0:T(8,128)S(1)} %add.18), channel_id=1, source_target_pairs={{0,8},{2,10},{4,12},{6,14},{8,0},{10,2},{12,4},{14,6},{1,9},{3,11}... | collective-permute-start | bytes 12296 | tf_op jit(solution)/shard_map/ppermute | solution.py:377
  133.9 6.0 %collective-permute-done.11 = f32[8,128]{1,0:T(8,128)S(1)} collective-permute-done((f32[8,128]{1,0:T(8,128)S(1)}, f32[8,128]{1,0:T(8,128)S(1)}, u32[]{:S(2)}, u32[]{:S(2)}) %collective-permute-start.11) | collective-permute-done | bytes 4128 | tf_op jit(solution)/shard_map/ppermute | solution.py:377
  140.5 4.9 %all-to-all-done.5 = bf16[16,64,768]{2,1,0:T(8,128)(2,1)S(1)} async-done(((bf16[16,64,768]{2,1,0:T(8,128)(2,1)}), bf16[16,64,768]{2,1,0:T(8,128)(2,1)S(1)}, u32[]{:S(2)}, u32[]{:S(2)}) %all-to-all-start.5) | async-done | bytes 1572896 | tf_op jit(solution)/shard_map/all_to_all | solution.py:369
  145.5 1.0 multiply_reduce_fusion
  (36 shorter events, 5.5 us)
Async XLA Ops:
  0.6 0.9 copy-start
  1.5 1.3 copy-start.1
  2.9 12.6 %copy-start.2 = (s32[64]{0:T(128)S(1)}, s32[64]{0:T(128)}, u32[]{:S(2)}) copy-start(s32[64]{0:T(128)} %param.7) | copy-start | bytes 772
  2.9 13.2 %copy-start.3 = (s32[128]{0:T(128)S(1)}, s32[128]{0:T(128)}, u32[]{:S(2)}) copy-start(s32[128]{0:T(128)} %param.6) | copy-start | bytes 1540
  2.9 16.0 %collective-permute-start.3 = (bf16[128,768]{1,0:T(8,128)(2,1)S(1)}, bf16[128,768]{1,0:T(8,128)(2,1)}, u32[]{:S(2)}, u32[]{:S(2)}) collective-permute-start(bf16[128,768]{1,0:T(8,128)(2,1)S(1)} %copy-done.1), channel_id=1, source_target_pairs={{0,12},{2,14},{4,0},{6,2},{8,4},{10,6},{12,8},{14,10},{1,13},{3,15... | collective-permute-start | bytes 589832 | tf_op jit(solution)/shard_map/ppermute | solution.py:314
  8.4 13.4 %collective-permute-start.2 = (bf16[128,768]{1,0:T(8,128)(2,1)S(1)}, bf16[128,768]{1,0:T(8,128)(2,1)S(1)}, u32[]{:S(2)}, u32[]{:S(2)}) collective-permute-start(bf16[128,768]{1,0:T(8,128)(2,1)S(1)} %copy-done.1), channel_id=1, source_target_pairs={{0,4},{2,6},{4,8},{6,10},{8,12},{10,14},{12,0},{14,2},{1,5},{3,7},... | collective-permute-start | bytes 589832 | tf_op jit(solution)/shard_map/ppermute | solution.py:314
  8.4 30.5 %all-to-all-start = ((bf16[16,64,768]{2,1,0:T(8,128)(2,1)}), bf16[16,64,768]{2,1,0:T(8,128)(2,1)S(1)}, u32[]{:S(2)}, u32[]{:S(2)}) async-start(bf16[16,64,768]{2,1,0:T(8,128)(2,1)} %shard_map.67), calls=%async_computation | async-start | bytes 3145728 | tf_op jit(solution)/shard_map/all_to_all | solution.py:324
  16.8 8.4 %collective-permute-start = (bf16[128,768]{1,0:T(8,128)(2,1)S(1)}, bf16[128,768]{1,0:T(8,128)(2,1)S(1)}, u32[]{:S(2)}, u32[]{:S(2)}) collective-permute-start(bf16[128,768]{1,0:T(8,128)(2,1)S(1)} %copy-done.1), channel_id=1, source_target_pairs={{0,2},{2,4},{4,6},{6,8},{8,10},{10,12},{12,14},{14,0},{1,3},{3,5},... | collective-permute-start | bytes 589832 | tf_op jit(solution)/shard_map/ppermute | solution.py:314
  17.9 7.8 %collective-permute-start.1 = (bf16[128,768]{1,0:T(8,128)(2,1)S(1)}, bf16[128,768]{1,0:T(8,128)(2,1)S(1)}, u32[]{:S(2)}, u32[]{:S(2)}) collective-permute-start(bf16[128,768]{1,0:T(8,128)(2,1)S(1)} %copy-done.1), channel_id=1, source_target_pairs={{0,14},{2,0},{4,2},{6,4},{8,6},{10,8},{12,10},{14,12},{1,15},{3,1}... | collective-permute-start | bytes 589832 | tf_op jit(solution)/shard_map/ppermute | solution.py:314
  18.9 9.0 %collective-permute-start.5 = (bf16[128,768]{1,0:T(8,128)(2,1)}, bf16[128,768]{1,0:T(8,128)(2,1)S(1)}, u32[]{:S(2)}, u32[]{:S(2)}) collective-permute-start(bf16[128,768]{1,0:T(8,128)(2,1)} %collective-permute-done.3), channel_id=1, source_target_pairs={{0,14},{2,0},{4,2},{6,4},{8,6},{10,8},{12,10},{14,12},{1,15},{3,1}... | collective-permute-start | bytes 589832 | tf_op jit(solution)/shard_map/ppermute | solution.py:314
  21.8 7.5 %collective-permute-start.4 = (bf16[128,768]{1,0:T(8,128)(2,1)S(1)}, bf16[128,768]{1,0:T(8,128)(2,1)S(1)}, u32[]{:S(2)}, u32[]{:S(2)}) collective-permute-start(bf16[128,768]{1,0:T(8,128)(2,1)S(1)} %collective-permute-done.2), channel_id=1, source_target_pairs={{0,2},{2,4},{4,6},{6,8},{8,10},{10,12},{12,14},{14,0},{1,3},{3,5},... | collective-permute-start | bytes 589832 | tf_op jit(solution)/shard_map/ppermute | solution.py:314
  28.0 7.7 %collective-permute-start.7 = (bf16[64,768]{1,0:T(8,128)(2,1)S(1)}, bf16[64,768]{1,0:T(8,128)(2,1)S(1)}, u32[]{:S(2)}, u32[]{:S(2)}) collective-permute-start(bf16[64,768]{1,0:T(8,128)(2,1)S(1)} %slice.13), channel_id=1, source_target_pairs={{0,14},{2,0},{4,2},{6,4},{8,6},{10,8},{12,10},{14,12},{1,15},{3,1}... | collective-permute-start | bytes 294920 | tf_op jit(solution)/shard_map/ppermute | solution.py:314
  29.3 6.3 %collective-permute-start.6 = (bf16[64,768]{1,0:T(8,128)(2,1)S(1)}, bf16[64,768]{1,0:T(8,128)(2,1)S(1)}, u32[]{:S(2)}, u32[]{:S(2)}) collective-permute-start(bf16[64,768]{1,0:T(8,128)(2,1)S(1)} %slice.12), channel_id=1, source_target_pairs={{0,2},{2,4},{4,6},{6,8},{8,10},{10,12},{12,14},{14,0},{1,3},{3,5},... | collective-permute-start | bytes 294920 | tf_op jit(solution)/shard_map/ppermute | solution.py:314
  38.9 3.4 %collective-permute-start.8 = (bf16[1024,768]{1,0:T(8,128)(2,1)S(1)}, bf16[1024,768]{1,0:T(8,128)(2,1)S(1)}, u32[]{:S(2)}, u32[]{:S(2)}) collective-permute-start(bf16[1024,768]{1,0:T(8,128)(2,1)S(1)} %constant_dynamic-update-slice_fusion.y_ref.ya_ref), channel_id=1, source_target_pairs={{0,16},{16,0},{1,17},{17,1},{2,18},{18,2},{3,19},{19,3},{4,20},{20... | collective-permute-start | bytes 4718600 | tf_op jit(solution)/shard_map/ppermute | solution.py:339
  119.9 25.5 %all-to-all-start.5 = ((bf16[16,64,768]{2,1,0:T(8,128)(2,1)}), bf16[16,64,768]{2,1,0:T(8,128)(2,1)S(1)}, u32[]{:S(2)}, u32[]{:S(2)}) async-start(bf16[16,64,768]{2,1,0:T(8,128)(2,1)} %bitcast.11), calls=%async_computation.5 | async-start | bytes 3145728 | tf_op jit(solution)/shard_map/all_to_all | solution.py:369
  124.3 3.6 %collective-permute-start.9 = (f32[8,128]{1,0:T(8,128)S(1)}, f32[8,128]{1,0:T(8,128)S(1)}, u32[]{:S(2)}, u32[]{:S(2)}) collective-permute-start(f32[8,128]{1,0:T(8,128)S(1)} %get-tuple-element.41), channel_id=1, source_target_pairs={{0,2},{2,0},{4,6},{6,4},{8,10},{10,8},{12,14},{14,12},{1,3},{3,1},... | collective-permute-start | bytes 12296 | tf_op jit(solution)/shard_map/ppermute | solution.py:377
  127.9 4.5 %collective-permute-start.10 = (f32[8,128]{1,0:T(8,128)S(1)}, f32[8,128]{1,0:T(8,128)S(1)}, u32[]{:S(2)}, u32[]{:S(2)}) collective-permute-start(f32[8,128]{1,0:T(8,128)S(1)} %add.17), channel_id=1, source_target_pairs={{0,4},{2,6},{4,0},{6,2},{8,12},{10,14},{12,8},{14,10},{1,5},{3,7},... | collective-permute-start | bytes 12296 | tf_op jit(solution)/shard_map/ppermute | solution.py:377
  132.4 7.5 %collective-permute-start.11 = (f32[8,128]{1,0:T(8,128)S(1)}, f32[8,128]{1,0:T(8,128)S(1)}, u32[]{:S(2)}, u32[]{:S(2)}) collective-permute-start(f32[8,128]{1,0:T(8,128)S(1)} %add.18), channel_id=1, source_target_pairs={{0,8},{2,10},{4,12},{6,14},{8,0},{10,2},{12,4},{14,6},{1,9},{3,11}... | collective-permute-start | bytes 12296 | tf_op jit(solution)/shard_map/ppermute | solution.py:377

commit v4 on v3

--- a/solution.py
+++ b/solution.py
@@ -329,9 +329,10 @@
         math.log2(domain_counts.shape[0]) - math.log2(total_cols)
     )
     mid = targets.shape[0] // 2
-    late, logb = lax.optimization_barrier((targets, logb))
-    near = [shift(late, 1), shift(late, -1), shift(targets, 2), shift(targets, -2)]
-    far = [shift(near[2], 1), shift(near[3], -1)]
+    two = [shift(targets, 2), shift(targets, -2)]
+    far = [shift(two[0], 1), shift(two[1], -1)]
+    late, *far = lax.optimization_barrier((targets, *far))
+    near = [shift(late, 1), shift(late, -1)] + two
     ends = [shift(far[0][:mid], 1), shift(far[1][mid:], -1)]
     ya = jnp.concatenate([targets] + near + far + ends, axis=0)
     scale = TO2 / width

time: 147 us -> 145 us (0.986)
    all_to_all x2, blocking collectives: 28.5 us -> 25.4 us  [columns(): return lax.all_to_all(out, TG, 0, 0, tiled=True)]
    ppermute x8, waiting for transfers between devices: 10.7 us -> 13 us  [shift(): lax.ppermute(block, 'z', [(i, (i + by) % depth) for i in range(depth)])]
    all_to_all x2, blocking collectives: 22.2 us -> 23.9 us  [columns(): parts = lax.all_to_all(out, CG, 0, 0, tiled=True)]
    all_to_all x1, waiting for transfers between devices: 3.23 us -> 1.65 us  [local(): x = lax.all_to_all(x, CG, 0, 0, tiled=True).reshape(rows, width)]
  transfers between devices with their start and end apart: 14 -> 14, of which waited for: 10 -> 12; matrix products, arithmetic and copies ran while one was open for 2% -> 1% of each run, Pallas kernels for 2% -> 2%
where the time goes in v4:
time: 145 us
  blocking collectives  60.6 us (42%)
  waiting for transfers between devices  33.4 us (23%)
  starting transfers between devices  26.2 us (18%)
  Pallas kernels  19.9 us (14%)
  other arithmetic  2.96 us (2%)
    all_to_all x2, blocking collectives, columns(): return lax.all_to_all(out, TG, 0, 0, tiled=True)  25.4 us
    all_to_all x2, blocking collectives, columns(): parts = lax.all_to_all(out, CG, 0, 0, tiled=True)  23.9 us
    pallas_call x8, Pallas kernels, run(): pl.pallas_call(kernel, in_specs=[special.get(i, VMEM) for i in range(len(...  19.9 us
    ppermute x8, waiting for transfers between devices, shift(): lax.ppermute(block, 'z', [(i, (i + by) % depth) for i in range(depth)])  13 us
    ppermute x3, waiting for transfers between devices, local(): cand = cand + lax.ppermute(cand, 'z', [(i, i ^ bit) for i in range(depth)])  12.9 us
    ppermute x8, starting transfers between devices, shift(): lax.ppermute(block, 'z', [(i, (i + by) % depth) for i in range(depth)])  12.7 us
    all_to_all x1, blocking collectives, local(): parts = lax.all_to_all(out, CG, 0, 0, tiled=True)  11.3 us
    all_to_all x1, starting transfers between devices, local(): x = lax.all_to_all(x, CG, 0, 0, tiled=True).reshape(rows, width)  7.03 us
  transfers between devices with their start and end apart: 14, of which 12 were waited for; matrix products, arithmetic and copies ran while one was open for 1% of the time, Pallas kernels for 2%

profile of v4, /device:TPU:32, one launch (start us, length us, event | category | flops | bytes accessed | tf_op | source)
XLA Modules:
  0.0 145.0 jit_solution(15597019242897427578)
XLA Ops:
  1.5 1.3 shard_map.67
  2.9 5.5 %collective-permute-start.2 = (bf16[128,768]{1,0:T(8,128)(2,1)S(1)}, bf16[128,768]{1,0:T(8,128)(2,1)S(1)}, u32[]{:S(2)}, u32[]{:S(2)}) collective-permute-start(bf16[128,768]{1,0:T(8,128)(2,1)S(1)} %copy-done.1), channel_id=1, source_target_pairs={{0,12},{2,14},{4,0},{6,2},{8,4},{10,6},{12,8},{14,10},{1,13},{3,15... | collective-permute-start | bytes 589832 | tf_op jit(solution)/shard_map/ppermute | solution.py:314
  8.4 7.0 %all-to-all-start = ((bf16[16,64,768]{2,1,0:T(8,128)(2,1)}), bf16[16,64,768]{2,1,0:T(8,128)(2,1)S(1)}, u32[]{:S(2)}, u32[]{:S(2)}) async-start(bf16[16,64,768]{2,1,0:T(8,128)(2,1)} %shard_map.67), calls=%async_computation | async-start | bytes 3145728 | tf_op jit(solution)/shard_map/all_to_all | solution.py:324
  15.4 2.3 %collective-permute-start.3 = (bf16[128,768]{1,0:T(8,128)(2,1)S(1)}, bf16[128,768]{1,0:T(8,128)(2,1)S(1)}, u32[]{:S(2)}, u32[]{:S(2)}) collective-permute-start(bf16[128,768]{1,0:T(8,128)(2,1)S(1)} %collective-permute-done.2), channel_id=1, source_target_pairs={{0,14},{2,0},{4,2},{6,4},{8,6},{10,8},{12,10},{14,12},{1,15},{3,1}... | collective-permute-start | bytes 589832 | tf_op jit(solution)/shard_map/ppermute | solution.py:314
  17.8 3.3 %collective-permute-done = bf16[128,768]{1,0:T(8,128)(2,1)S(1)} collective-permute-done((bf16[128,768]{1,0:T(8,128)(2,1)S(1)}, bf16[128,768]{1,0:T(8,128)(2,1)S(1)}, u32[]{:S(2)}, u32[]{:S(2)}) %collective-permute-start) | collective-permute-done | bytes 196640 | tf_op jit(solution)/shard_map/ppermute | solution.py:314
  21.7 1.1 collective-permute-done.3
  22.9 4.2 %collective-permute-done.1 = bf16[128,768]{1,0:T(8,128)(2,1)S(1)} collective-permute-done((bf16[128,768]{1,0:T(8,128)(2,1)S(1)}, bf16[128,768]{1,0:T(8,128)(2,1)S(1)}, u32[]{:S(2)}, u32[]{:S(2)}) %collective-permute-start.1) | collective-permute-done | bytes 196640 | tf_op jit(solution)/shard_map/ppermute | solution.py:314
  28.0 1.8 %collective-permute-start.5 = (bf16[128,768]{1,0:T(8,128)(2,1)S(1)}, bf16[128,768]{1,0:T(8,128)(2,1)S(1)}, u32[]{:S(2)}, u32[]{:S(2)}) collective-permute-start(bf16[128,768]{1,0:T(8,128)(2,1)S(1)} %copy-done.1), channel_id=1, source_target_pairs={{0,14},{2,0},{4,2},{6,4},{8,6},{10,8},{12,10},{14,12},{1,15},{3,1}... | collective-permute-start | bytes 589832 | tf_op jit(solution)/shard_map/ppermute | solution.py:314
  29.8 2.7 %collective-permute-start.7 = (bf16[64,768]{1,0:T(8,128)(2,1)S(1)}, bf16[64,768]{1,0:T(8,128)(2,1)S(1)}, u32[]{:S(2)}, u32[]{:S(2)}) collective-permute-start(bf16[64,768]{1,0:T(8,128)(2,1)S(1)} %slice.10), channel_id=1, source_target_pairs={{0,14},{2,0},{4,2},{6,4},{8,6},{10,8},{12,10},{14,12},{1,15},{3,1}... | collective-permute-start | bytes 294920 | tf_op jit(solution)/shard_map/ppermute | solution.py:314
  32.6 1.0 collective-permute-done.4
  34.3 2.9 %collective-permute-done.6 = bf16[64,768]{1,0:T(8,128)(2,1)S(1)} collective-permute-done((bf16[64,768]{1,0:T(8,128)(2,1)S(1)}, bf16[64,768]{1,0:T(8,128)(2,1)S(1)}, u32[]{:S(2)}, u32[]{:S(2)}) %collective-permute-start.6) | collective-permute-done | bytes 98336 | tf_op jit(solution)/shard_map/ppermute | solution.py:314
  37.3 1.7 %all-to-all-done = bf16[16,64,768]{2,1,0:T(8,128)(2,1)S(1)} async-done(((bf16[16,64,768]{2,1,0:T(8,128)(2,1)}), bf16[16,64,768]{2,1,0:T(8,128)(2,1)S(1)}, u32[]{:S(2)}, u32[]{:S(2)}) %all-to-all-start) | async-done | bytes 1572896 | tf_op jit(solution)/shard_map/all_to_all | solution.py:324
  38.9 2.4 %shard_map.68 = (f32[1024,1024]{1,0:T(8,128)S(1)}, f32[1024,128]{1,0:T(8,128)S(1)}, f32[1024,128]{1,0:T(8,128)S(1)}, f32[1024,128]{1,0:T(8,128)S(1)}) custom-call(bf16[1024,768]{1,0:T(8,128)(2,1)S(1)} %bitcast.8, bf16[1024,768]{1,0:T(8,128)(2,1)S(1)} %constant_dynamic-update-slice_fusion.y_ref.ya_ref), custom_call_target="tpu_custom_call" | custom-call | flops 1610612736 | bytes 8388608 | tf_op jit(solution)/shard_map/pallas_call | solution.py:303
  41.3 1.0 collective-permute-done.8.y_ref.yb_ref
  42.3 2.5 %shard_map.69 = (f32[1024,1024]{1,0:T(8,128)S(1)}, f32[16,8,128]{2,1,0:T(8,128)S(1)}) custom-call(bf16[1024,768]{1,0:T(8,128)(2,1)S(1)} %bitcast.9, f32[1024,128]{1,0:T(8,128)S(1)} %get-tuple-element.31.sqx_ref, bf16[1024,768]{1,0:T(8,128)(2,1)S(1)} %collective-permute-done.8.y_ref.yb_ref, f32[1024,128]{1,0:T(8,128)S(1)} %get-tuple-element.32.m0_ref, ...), custom_call_target="tpu_custom_call" | custom-call | flops 1610612736 | bytes 8388608 | tf_op jit(solution)/shard_map/pallas_call | solution.py:303
  44.8 13.0 %all_to_all.35.parts_ref = f32[16,8,128]{2,1,0:T(8,128)S(1)} all-to-all(f32[16,8,128]{2,1,0:T(8,128)S(1)} %get-tuple-element.34), channel_id=1, replica_groups=mesh['xl'=2,'y'=4,'core'=2,'z'=8,'xh'=2] {'xh','xl','y'}, dimensions={0} | all-to-all | bytes 131072 | tf_op jit(solution)/shard_map/all_to_all | solution.py:356
  57.8 2.5 %shard_map.70 = f32[16,24,128]{2,1,0:T(8,128)S(1)} custom-call(f32[16,8,128]{2,1,0:T(8,128)S(1)} %all_to_all.35.parts_ref, f32[1024,1024]{1,0:T(8,128)S(1)} %get-tuple-element.35.ca_ref, f32[1024,1024]{1,0:T(8,128)S(1)} %get-tuple-element.36.cb_ref, f32[1,128]{1,0:T(1,128)S(1)} %add_bitcast_fusion.1.refs_0_), custom_call_target="tpu_custom_call" | custom-call | flops 1610612736 | bytes 8388608 | tf_op jit(solution)/shard_map/pallas_call | solution.py:303
  60.3 13.8 %all_to_all.36.parts_ref = f32[16,24,128]{2,1,0:T(8,128)S(1)} all-to-all(f32[16,24,128]{2,1,0:T(8,128)S(1)} %shard_map.70), channel_id=1, replica_groups=mesh['xl'=2,'y'=4,'core'=2,'z'=8,'xh'=2] {'core','z'}, dimensions={0} | all-to-all | bytes 393216 | tf_op jit(solution)/shard_map/all_to_all | solution.py:358
  74.1 2.4 %shard_map.71 = (f32[16,8,128]{2,1,0:T(8,128)S(1)}, f32[16,128]{1,0:T(8,128)S(1)}) custom-call(f32[16,24,128]{2,1,0:T(8,128)S(1)} %all_to_all.36.parts_ref, f32[1024,1024]{1,0:T(8,128)S(1)} %get-tuple-element.35.ca_ref, f32[1024,1024]{1,0:T(8,128)S(1)} %get-tuple-element.36.cb_ref), custom_call_target="tpu_custom_call" | custom-call | flops 1610612736 | bytes 8388608 | tf_op jit(solution)/shard_map/pallas_call | solution.py:303
  76.5 10.9 %all_to_all.37.parts_ref = f32[16,8,128]{2,1,0:T(8,128)S(1)} all-to-all(f32[16,8,128]{2,1,0:T(8,128)S(1)} %get-tuple-element.38), channel_id=1, replica_groups=mesh['xl'=2,'y'=4,'core'=2,'z'=8,'xh'=2] {'xh','xl','y'}, dimensions={0} | all-to-all | bytes 131072 | tf_op jit(solution)/shard_map/all_to_all | solution.py:356
  87.4 2.5 %shard_map.72 = f32[16,16,128]{2,1,0:T(8,128)S(1)} custom-call(f32[16,8,128]{2,1,0:T(8,128)S(1)} %all_to_all.37.parts_ref, f32[1024,1024]{1,0:T(8,128)S(1)} %get-tuple-element.35.ca_ref, f32[1024,1024]{1,0:T(8,128)S(1)} %get-tuple-element.36.cb_ref), custom_call_target="tpu_custom_call" | custom-call | flops 1610612736 | bytes 8388608 | tf_op jit(solution)/shard_map/pallas_call | solution.py:303
  89.9 11.6 %all_to_all.38.parts_ref = f32[16,16,128]{2,1,0:T(8,128)S(1)} all-to-all(f32[16,16,128]{2,1,0:T(8,128)S(1)} %shard_map.72), channel_id=1, replica_groups=mesh['xl'=2,'y'=4,'core'=2,'z'=8,'xh'=2] {'core','z'}, dimensions={0} | all-to-all | bytes 262144 | tf_op jit(solution)/shard_map/all_to_all | solution.py:358
  101.5 5.7 %shard_map.73 = (f32[16,24,128]{2,1,0:T(8,128)S(1)}, bf16[1024,768]{1,0:T(8,128)(2,1)}) custom-call(f32[16,16,128]{2,1,0:T(8,128)S(1)} %all_to_all.38.parts_ref, f32[16,128]{1,0:T(8,128)S(1)} %get-tuple-element.39.logb_ref, f32[1024,1024]{1,0:T(8,128)S(1)} %get-tuple-element.35.ca_ref, f32[1024,1024]{1,0:T(8,128)S(1)} %get-tuple-element.36.cb_ref, ...), custom_call_target="tpu_custom_call" | custom-call | flops 1610612736 | bytes 8388608 | tf_op jit(solution)/shard_map/pallas_call | solution.py:303
  107.2 11.3 %all_to_all.39.parts_ref = f32[16,24,128]{2,1,0:T(8,128)S(1)} all-to-all(f32[16,24,128]{2,1,0:T(8,128)S(1)} %get-tuple-element.41), channel_id=1, replica_groups=mesh['xl'=2,'y'=4,'core'=2,'z'=8,'xh'=2] {'xh','xl','y'}, dimensions={0} | all-to-all | bytes 393216 | tf_op jit(solution)/shard_map/all_to_all | solution.py:369
  118.5 3.7 %all-to-all-start.5 = ((bf16[16,64,768]{2,1,0:T(8,128)(2,1)}), bf16[16,64,768]{2,1,0:T(8,128)(2,1)S(1)}, u32[]{:S(2)}, u32[]{:S(2)}) async-start(bf16[16,64,768]{2,1,0:T(8,128)(2,1)} %bitcast.11), calls=%async_computation.5 | async-start | bytes 3145728 | tf_op jit(solution)/shard_map/all_to_all | solution.py:370
  123.2 3.3 %collective-permute-done.9 = f32[8,128]{1,0:T(8,128)S(1)} collective-permute-done((f32[8,128]{1,0:T(8,128)S(1)}, f32[8,128]{1,0:T(8,128)S(1)}, u32[]{:S(2)}, u32[]{:S(2)}) %collective-permute-start.9) | collective-permute-done | bytes 4128 | tf_op jit(solution)/shard_map/ppermute | solution.py:378
  126.5 0.9 collective-permute-start.10
  127.4 3.6 %collective-permute-done.10 = f32[8,128]{1,0:T(8,128)S(1)} collective-permute-done((f32[8,128]{1,0:T(8,128)S(1)}, f32[8,128]{1,0:T(8,128)S(1)}, u32[]{:S(2)}, u32[]{:S(2)}) %collective-permute-start.10) | collective-permute-done | bytes 4128 | tf_op jit(solution)/shard_map/ppermute | solution.py:378
  131.0 1.5 %collective-permute-start.11 = (f32[8,128]{1,0:T(8,128)S(1)}, f32[8,128]{1,0:T(8,128)S(1)}, u32[]{:S(2)}, u32[]{:S(2)}) collective-permute-start(f32[8,128]{1,0:T(8,128)S(1)} %add.29), channel_id=1, source_target_pairs={{0,8},{2,10},{4,12},{6,14},{8,0},{10,2},{12,4},{14,6},{1,9},{3,11}... | collective-permute-start | bytes 12296 | tf_op jit(solution)/shard_map/ppermute | solution.py:378
  132.5 6.0 %collective-permute-done.11 = f32[8,128]{1,0:T(8,128)S(1)} collective-permute-done((f32[8,128]{1,0:T(8,128)S(1)}, f32[8,128]{1,0:T(8,128)S(1)}, u32[]{:S(2)}, u32[]{:S(2)}) %collective-permute-start.11) | collective-permute-done | bytes 4128 | tf_op jit(solution)/shard_map/ppermute | solution.py:378
  139.1 4.9 %all-to-all-done.5 = bf16[16,64,768]{2,1,0:T(8,128)(2,1)S(1)} async-done(((bf16[16,64,768]{2,1,0:T(8,128)(2,1)}), bf16[16,64,768]{2,1,0:T(8,128)(2,1)S(1)}, u32[]{:S(2)}, u32[]{:S(2)}) %all-to-all-start.5) | async-done | bytes 1572896 | tf_op jit(solution)/shard_map/all_to_all | solution.py:370
  144.0 1.0 multiply_reduce_fusion
  (40 shorter events, 4.8 us)
Async XLA Ops:
  0.6 0.9 copy-start
  1.5 1.3 copy-start.1
  2.9 12.6 %copy-start.4 = (s32[64]{0:T(128)S(1)}, s32[64]{0:T(128)}, u32[]{:S(2)}) copy-start(s32[64]{0:T(128)} %param.7) | copy-start | bytes 772
  2.9 18.8 %copy-start.5 = (s32[128]{0:T(128)S(1)}, s32[128]{0:T(128)}, u32[]{:S(2)}) copy-start(s32[128]{0:T(128)} %param.6) | copy-start | bytes 1540
  2.9 12.5 %collective-permute-start.2 = (bf16[128,768]{1,0:T(8,128)(2,1)S(1)}, bf16[128,768]{1,0:T(8,128)(2,1)S(1)}, u32[]{:S(2)}, u32[]{:S(2)}) collective-permute-start(bf16[128,768]{1,0:T(8,128)(2,1)S(1)} %copy-done.1), channel_id=1, source_target_pairs={{0,12},{2,14},{4,0},{6,2},{8,4},{10,6},{12,8},{14,10},{1,13},{3,15... | collective-permute-start | bytes 589832 | tf_op jit(solution)/shard_map/ppermute | solution.py:314
  8.4 12.7 %collective-permute-start = (bf16[128,768]{1,0:T(8,128)(2,1)S(1)}, bf16[128,768]{1,0:T(8,128)(2,1)S(1)}, u32[]{:S(2)}, u32[]{:S(2)}) collective-permute-start(bf16[128,768]{1,0:T(8,128)(2,1)S(1)} %copy-done.1), channel_id=1, source_target_pairs={{0,4},{2,6},{4,8},{6,10},{8,12},{10,14},{12,0},{14,2},{1,5},{3,7},... | collective-permute-start | bytes 589832 | tf_op jit(solution)/shard_map/ppermute | solution.py:314
  8.4 30.5 %all-to-all-start = ((bf16[16,64,768]{2,1,0:T(8,128)(2,1)}), bf16[16,64,768]{2,1,0:T(8,128)(2,1)S(1)}, u32[]{:S(2)}, u32[]{:S(2)}) async-start(bf16[16,64,768]{2,1,0:T(8,128)(2,1)} %shard_map.67), calls=%async_computation | async-start | bytes 3145728 | tf_op jit(solution)/shard_map/all_to_all | solution.py:324
  15.4 7.4 %collective-permute-start.3 = (bf16[128,768]{1,0:T(8,128)(2,1)S(1)}, bf16[128,768]{1,0:T(8,128)(2,1)S(1)}, u32[]{:S(2)}, u32[]{:S(2)}) collective-permute-start(bf16[128,768]{1,0:T(8,128)(2,1)S(1)} %collective-permute-done.2), channel_id=1, source_target_pairs={{0,14},{2,0},{4,2},{6,4},{8,6},{10,8},{12,10},{14,12},{1,15},{3,1}... | collective-permute-start | bytes 589832 | tf_op jit(solution)/shard_map/ppermute | solution.py:314
  21.0 6.9 %copy-start.2 = (bf16[128,768]{1,0:T(8,128)(2,1)}, bf16[128,768]{1,0:T(8,128)(2,1)S(1)}, u32[]{:S(2)}) copy-start(bf16[128,768]{1,0:T(8,128)(2,1)S(1)} %collective-permute-done) | copy-start | bytes 589828
  21.0 6.0 %collective-permute-start.1 = (bf16[128,768]{1,0:T(8,128)(2,1)S(1)}, bf16[128,768]{1,0:T(8,128)(2,1)S(1)}, u32[]{:S(2)}, u32[]{:S(2)}) collective-permute-start(bf16[128,768]{1,0:T(8,128)(2,1)S(1)} %collective-permute-done), channel_id=1, source_target_pairs={{0,2},{2,4},{4,6},{6,8},{8,10},{10,12},{12,14},{14,0},{1,3},{3,5},... | collective-permute-start | bytes 589832 | tf_op jit(solution)/shard_map/ppermute | solution.py:314
  27.0 6.6 %collective-permute-start.4 = (bf16[128,768]{1,0:T(8,128)(2,1)S(1)}, bf16[128,768]{1,0:T(8,128)(2,1)S(1)}, u32[]{:S(2)}, u32[]{:S(2)}) collective-permute-start(bf16[128,768]{1,0:T(8,128)(2,1)S(1)} %copy-done.1), channel_id=1, source_target_pairs={{0,2},{2,4},{4,6},{6,8},{8,10},{10,12},{12,14},{14,0},{1,3},{3,5},... | collective-permute-start | bytes 589832 | tf_op jit(solution)/shard_map/ppermute | solution.py:314
  28.0 6.2 %collective-permute-start.5 = (bf16[128,768]{1,0:T(8,128)(2,1)S(1)}, bf16[128,768]{1,0:T(8,128)(2,1)S(1)}, u32[]{:S(2)}, u32[]{:S(2)}) collective-permute-start(bf16[128,768]{1,0:T(8,128)(2,1)S(1)} %copy-done.1), channel_id=1, source_target_pairs={{0,14},{2,0},{4,2},{6,4},{8,6},{10,8},{12,10},{14,12},{1,15},{3,1}... | collective-permute-start | bytes 589832 | tf_op jit(solution)/shard_map/ppermute | solution.py:314
  29.8 4.4 %copy-start.3 = (bf16[128,768]{1,0:T(8,128)(2,1)S(1)}, bf16[128,768]{1,0:T(8,128)(2,1)}, u32[]{:S(2)}) copy-start(bf16[128,768]{1,0:T(8,128)(2,1)} %copy-done.2) | copy-start | bytes 589828
  29.8 7.4 %collective-permute-start.7 = (bf16[64,768]{1,0:T(8,128)(2,1)S(1)}, bf16[64,768]{1,0:T(8,128)(2,1)S(1)}, u32[]{:S(2)}, u32[]{:S(2)}) collective-permute-start(bf16[64,768]{1,0:T(8,128)(2,1)S(1)} %slice.10), channel_id=1, source_target_pairs={{0,14},{2,0},{4,2},{6,4},{8,6},{10,8},{12,10},{14,12},{1,15},{3,1}... | collective-permute-start | bytes 294920 | tf_op jit(solution)/shard_map/ppermute | solution.py:314
  32.6 4.6 %collective-permute-start.6 = (bf16[64,768]{1,0:T(8,128)(2,1)S(1)}, bf16[64,768]{1,0:T(8,128)(2,1)S(1)}, u32[]{:S(2)}, u32[]{:S(2)}) collective-permute-start(bf16[64,768]{1,0:T(8,128)(2,1)S(1)} %slice.9), channel_id=1, source_target_pairs={{0,2},{2,4},{4,6},{6,8},{8,10},{10,12},{12,14},{14,0},{1,3},{3,5},... | collective-permute-start | bytes 294920 | tf_op jit(solution)/shard_map/ppermute | solution.py:314
  38.9 3.4 %collective-permute-start.8 = (bf16[1024,768]{1,0:T(8,128)(2,1)S(1)}, bf16[1024,768]{1,0:T(8,128)(2,1)S(1)}, u32[]{:S(2)}, u32[]{:S(2)}) collective-permute-start(bf16[1024,768]{1,0:T(8,128)(2,1)S(1)} %constant_dynamic-update-slice_fusion.y_ref.ya_ref), channel_id=1, source_target_pairs={{0,16},{16,0},{1,17},{17,1},{2,18},{18,2},{3,19},{19,3},{4,20},{20... | collective-permute-start | bytes 4718600 | tf_op jit(solution)/shard_map/ppermute | solution.py:340
  118.5 25.5 %all-to-all-start.5 = ((bf16[16,64,768]{2,1,0:T(8,128)(2,1)}), bf16[16,64,768]{2,1,0:T(8,128)(2,1)S(1)}, u32[]{:S(2)}, u32[]{:S(2)}) async-start(bf16[16,64,768]{2,1,0:T(8,128)(2,1)} %bitcast.11), calls=%async_computation.5 | async-start | bytes 3145728 | tf_op jit(solution)/shard_map/all_to_all | solution.py:370
  122.9 3.6 %collective-permute-start.9 = (f32[8,128]{1,0:T(8,128)S(1)}, f32[8,128]{1,0:T(8,128)S(1)}, u32[]{:S(2)}, u32[]{:S(2)}) collective-permute-start(f32[8,128]{1,0:T(8,128)S(1)} %get-tuple-element.43), channel_id=1, source_target_pairs={{0,2},{2,0},{4,6},{6,4},{8,10},{10,8},{12,14},{14,12},{1,3},{3,1},... | collective-permute-start | bytes 12296 | tf_op jit(solution)/shard_map/ppermute | solution.py:378
  126.5 4.5 %collective-permute-start.10 = (f32[8,128]{1,0:T(8,128)S(1)}, f32[8,128]{1,0:T(8,128)S(1)}, u32[]{:S(2)}, u32[]{:S(2)}) collective-permute-start(f32[8,128]{1,0:T(8,128)S(1)} %add.28), channel_id=1, source_target_pairs={{0,4},{2,6},{4,0},{6,2},{8,12},{10,14},{12,8},{14,10},{1,5},{3,7},... | collective-permute-start | bytes 12296 | tf_op jit(solution)/shard_map/ppermute | solution.py:378
  131.0 7.5 %collective-permute-start.11 = (f32[8,128]{1,0:T(8,128)S(1)}, f32[8,128]{1,0:T(8,128)S(1)}, u32[]{:S(2)}, u32[]{:S(2)}) collective-permute-start(f32[8,128]{1,0:T(8,128)S(1)} %add.29), channel_id=1, source_target_pairs={{0,8},{2,10},{4,12},{6,14},{8,0},{10,2},{12,4},{14,6},{1,9},{3,11}... | collective-permute-start | bytes 12296 | tf_op jit(solution)/shard_map/ppermute | solution.py:378

commit v5 on v4

--- a/solution.py
+++ b/solution.py
@@ -150,10 +150,10 @@
                 r = pl.multiple_of(i * sub, sub)
                 return tuple(a + jnp.exp2(score(r, k) - b) for a, b, k in zip(l, m, ks))
 
-            m = lax.fori_loop(1, rows // sub, top_step, tuple(score(0, k) for k in ks), unroll=4)
+            m = lax.fori_loop(1, rows // sub, top_step, tuple(score(0, k) for k in ks), unroll=8)
             zero = jnp.zeros((sub, LANE), jnp.float32)
             l = lax.fori_loop(
-                0, rows // sub, functools.partial(sum_step, m), (zero,) * group, unroll=4
+                0, rows // sub, functools.partial(sum_step, m), (zero,) * group, unroll=8
             )
             for a, b, k in zip(l, m, ks):
                 top = jnp.max(b, axis=0, keepdims=True)

time: 145 us -> 145 us (level)
  no operation moved by 1% of the time
where the time goes in v5:
time: 145 us
  blocking collectives  60.6 us (42%)
  waiting for transfers between devices  33.4 us (23%)
  starting transfers between devices  26.2 us (18%)
  Pallas kernels  19.7 us (14%)
  other arithmetic  2.96 us (2%)
    all_to_all x2, blocking collectives, columns(): return lax.all_to_all(out, TG, 0, 0, tiled=True)  25.4 us
    all_to_all x2, blocking collectives, columns(): parts = lax.all_to_all(out, CG, 0, 0, tiled=True)  23.9 us
    pallas_call x8, Pallas kernels, run(): pl.pallas_call(kernel, in_specs=[special.get(i, VMEM) for i in range(len(...  19.7 us
    ppermute x8, waiting for transfers between devices, shift(): lax.ppermute(block, 'z', [(i, (i + by) % depth) for i in range(depth)])  13 us
    ppermute x3, waiting for transfers between devices, local(): cand = cand + lax.ppermute(cand, 'z', [(i, i ^ bit) for i in range(depth)])  12.9 us
    ppermute x8, starting transfers between devices, shift(): lax.ppermute(block, 'z', [(i, (i + by) % depth) for i in range(depth)])  12.7 us
    all_to_all x1, blocking collectives, local(): parts = lax.all_to_all(out, CG, 0, 0, tiled=True)  11.3 us
    all_to_all x1, starting transfers between devices, local(): x = lax.all_to_all(x, CG, 0, 0, tiled=True).reshape(rows, width)  7.03 us
  transfers between devices with their start and end apart: 14, of which 12 were waited for; matrix products, arithmetic and copies ran while one was open for 1% of the time, Pallas kernels for 2%

profile of v5, /device:TPU:32, one launch (start us, length us, event | category | flops | bytes accessed | tf_op | source)
XLA Modules:
  0.0 144.8 jit_solution(431330232543706741)
XLA Ops:
  1.5 1.3 shard_map.67
  2.9 5.5 %collective-permute-start.2 = (bf16[128,768]{1,0:T(8,128)(2,1)S(1)}, bf16[128,768]{1,0:T(8,128)(2,1)S(1)}, u32[]{:S(2)}, u32[]{:S(2)}) collective-permute-start(bf16[128,768]{1,0:T(8,128)(2,1)S(1)} %copy-done.1), channel_id=1, source_target_pairs={{0,12},{2,14},{4,0},{6,2},{8,4},{10,6},{12,8},{14,10},{1,13},{3,15... | collective-permute-start | bytes 589832 | tf_op jit(solution)/shard_map/ppermute | solution.py:314
  8.4 7.0 %all-to-all-start = ((bf16[16,64,768]{2,1,0:T(8,128)(2,1)}), bf16[16,64,768]{2,1,0:T(8,128)(2,1)S(1)}, u32[]{:S(2)}, u32[]{:S(2)}) async-start(bf16[16,64,768]{2,1,0:T(8,128)(2,1)} %shard_map.67), calls=%async_computation | async-start | bytes 3145728 | tf_op jit(solution)/shard_map/all_to_all | solution.py:324
  15.4 2.3 %collective-permute-start.3 = (bf16[128,768]{1,0:T(8,128)(2,1)S(1)}, bf16[128,768]{1,0:T(8,128)(2,1)S(1)}, u32[]{:S(2)}, u32[]{:S(2)}) collective-permute-start(bf16[128,768]{1,0:T(8,128)(2,1)S(1)} %collective-permute-done.2), channel_id=1, source_target_pairs={{0,14},{2,0},{4,2},{6,4},{8,6},{10,8},{12,10},{14,12},{1,15},{3,1}... | collective-permute-start | bytes 589832 | tf_op jit(solution)/shard_map/ppermute | solution.py:314
  17.8 3.3 %collective-permute-done = bf16[128,768]{1,0:T(8,128)(2,1)S(1)} collective-permute-done((bf16[128,768]{1,0:T(8,128)(2,1)S(1)}, bf16[128,768]{1,0:T(8,128)(2,1)S(1)}, u32[]{:S(2)}, u32[]{:S(2)}) %collective-permute-start) | collective-permute-done | bytes 196640 | tf_op jit(solution)/shard_map/ppermute | solution.py:314
  21.7 1.1 collective-permute-done.3
  22.9 4.2 %collective-permute-done.1 = bf16[128,768]{1,0:T(8,128)(2,1)S(1)} collective-permute-done((bf16[128,768]{1,0:T(8,128)(2,1)S(1)}, bf16[128,768]{1,0:T(8,128)(2,1)S(1)}, u32[]{:S(2)}, u32[]{:S(2)}) %collective-permute-start.1) | collective-permute-done | bytes 196640 | tf_op jit(solution)/shard_map/ppermute | solution.py:314
  28.0 1.8 %collective-permute-start.5 = (bf16[128,768]{1,0:T(8,128)(2,1)S(1)}, bf16[128,768]{1,0:T(8,128)(2,1)S(1)}, u32[]{:S(2)}, u32[]{:S(2)}) collective-permute-start(bf16[128,768]{1,0:T(8,128)(2,1)S(1)} %copy-done.1), channel_id=1, source_target_pairs={{0,14},{2,0},{4,2},{6,4},{8,6},{10,8},{12,10},{14,12},{1,15},{3,1}... | collective-permute-start | bytes 589832 | tf_op jit(solution)/shard_map/ppermute | solution.py:314
  29.8 2.7 %collective-permute-start.7 = (bf16[64,768]{1,0:T(8,128)(2,1)S(1)}, bf16[64,768]{1,0:T(8,128)(2,1)S(1)}, u32[]{:S(2)}, u32[]{:S(2)}) collective-permute-start(bf16[64,768]{1,0:T(8,128)(2,1)S(1)} %slice.10), channel_id=1, source_target_pairs={{0,14},{2,0},{4,2},{6,4},{8,6},{10,8},{12,10},{14,12},{1,15},{3,1}... | collective-permute-start | bytes 294920 | tf_op jit(solution)/shard_map/ppermute | solution.py:314
  32.6 1.0 collective-permute-done.4
  34.3 2.9 %collective-permute-done.6 = bf16[64,768]{1,0:T(8,128)(2,1)S(1)} collective-permute-done((bf16[64,768]{1,0:T(8,128)(2,1)S(1)}, bf16[64,768]{1,0:T(8,128)(2,1)S(1)}, u32[]{:S(2)}, u32[]{:S(2)}) %collective-permute-start.6) | collective-permute-done | bytes 98336 | tf_op jit(solution)/shard_map/ppermute | solution.py:314
  37.3 1.7 %all-to-all-done = bf16[16,64,768]{2,1,0:T(8,128)(2,1)S(1)} async-done(((bf16[16,64,768]{2,1,0:T(8,128)(2,1)}), bf16[16,64,768]{2,1,0:T(8,128)(2,1)S(1)}, u32[]{:S(2)}, u32[]{:S(2)}) %all-to-all-start) | async-done | bytes 1572896 | tf_op jit(solution)/shard_map/all_to_all | solution.py:324
  38.9 2.4 %shard_map.68 = (f32[1024,1024]{1,0:T(8,128)S(1)}, f32[1024,128]{1,0:T(8,128)S(1)}, f32[1024,128]{1,0:T(8,128)S(1)}, f32[1024,128]{1,0:T(8,128)S(1)}) custom-call(bf16[1024,768]{1,0:T(8,128)(2,1)S(1)} %bitcast.8, bf16[1024,768]{1,0:T(8,128)(2,1)S(1)} %constant_dynamic-update-slice_fusion.y_ref.ya_ref), custom_call_target="tpu_custom_call" | custom-call | flops 1610612736 | bytes 8388608 | tf_op jit(solution)/shard_map/pallas_call | solution.py:303
  41.3 1.0 collective-permute-done.8.y_ref.yb_ref
  42.3 2.5 %shard_map.69 = (f32[1024,1024]{1,0:T(8,128)S(1)}, f32[16,8,128]{2,1,0:T(8,128)S(1)}) custom-call(bf16[1024,768]{1,0:T(8,128)(2,1)S(1)} %bitcast.9, f32[1024,128]{1,0:T(8,128)S(1)} %get-tuple-element.31.sqx_ref, bf16[1024,768]{1,0:T(8,128)(2,1)S(1)} %collective-permute-done.8.y_ref.yb_ref, f32[1024,128]{1,0:T(8,128)S(1)} %get-tuple-element.32.m0_ref, ...), custom_call_target="tpu_custom_call" | custom-call | flops 1610612736 | bytes 8388608 | tf_op jit(solution)/shard_map/pallas_call | solution.py:303
  44.8 13.0 %all_to_all.35.parts_ref = f32[16,8,128]{2,1,0:T(8,128)S(1)} all-to-all(f32[16,8,128]{2,1,0:T(8,128)S(1)} %get-tuple-element.34), channel_id=1, replica_groups=mesh['xl'=2,'y'=4,'core'=2,'z'=8,'xh'=2] {'xh','xl','y'}, dimensions={0} | all-to-all | bytes 131072 | tf_op jit(solution)/shard_map/all_to_all | solution.py:356
  57.8 2.4 %shard_map.70 = f32[16,24,128]{2,1,0:T(8,128)S(1)} custom-call(f32[16,8,128]{2,1,0:T(8,128)S(1)} %all_to_all.35.parts_ref, f32[1024,1024]{1,0:T(8,128)S(1)} %get-tuple-element.35.ca_ref, f32[1024,1024]{1,0:T(8,128)S(1)} %get-tuple-element.36.cb_ref, f32[1,128]{1,0:T(1,128)S(1)} %add_bitcast_fusion.1.refs_0_), custom_call_target="tpu_custom_call" | custom-call | flops 1610612736 | bytes 8388608 | tf_op jit(solution)/shard_map/pallas_call | solution.py:303
  60.2 13.8 %all_to_all.36.parts_ref = f32[16,24,128]{2,1,0:T(8,128)S(1)} all-to-all(f32[16,24,128]{2,1,0:T(8,128)S(1)} %shard_map.70), channel_id=1, replica_groups=mesh['xl'=2,'y'=4,'core'=2,'z'=8,'xh'=2] {'core','z'}, dimensions={0} | all-to-all | bytes 393216 | tf_op jit(solution)/shard_map/all_to_all | solution.py:358
  74.0 2.4 %shard_map.71 = (f32[16,8,128]{2,1,0:T(8,128)S(1)}, f32[16,128]{1,0:T(8,128)S(1)}) custom-call(f32[16,24,128]{2,1,0:T(8,128)S(1)} %all_to_all.36.parts_ref, f32[1024,1024]{1,0:T(8,128)S(1)} %get-tuple-element.35.ca_ref, f32[1024,1024]{1,0:T(8,128)S(1)} %get-tuple-element.36.cb_ref), custom_call_target="tpu_custom_call" | custom-call | flops 1610612736 | bytes 8388608 | tf_op jit(solution)/shard_map/pallas_call | solution.py:303
  76.4 10.9 %all_to_all.37.parts_ref = f32[16,8,128]{2,1,0:T(8,128)S(1)} all-to-all(f32[16,8,128]{2,1,0:T(8,128)S(1)} %get-tuple-element.38), channel_id=1, replica_groups=mesh['xl'=2,'y'=4,'core'=2,'z'=8,'xh'=2] {'xh','xl','y'}, dimensions={0} | all-to-all | bytes 131072 | tf_op jit(solution)/shard_map/all_to_all | solution.py:356
  87.3 2.4 %shard_map.72 = f32[16,16,128]{2,1,0:T(8,128)S(1)} custom-call(f32[16,8,128]{2,1,0:T(8,128)S(1)} %all_to_all.37.parts_ref, f32[1024,1024]{1,0:T(8,128)S(1)} %get-tuple-element.35.ca_ref, f32[1024,1024]{1,0:T(8,128)S(1)} %get-tuple-element.36.cb_ref), custom_call_target="tpu_custom_call" | custom-call | flops 1610612736 | bytes 8388608 | tf_op jit(solution)/shard_map/pallas_call | solution.py:303
  89.7 11.6 %all_to_all.38.parts_ref = f32[16,16,128]{2,1,0:T(8,128)S(1)} all-to-all(f32[16,16,128]{2,1,0:T(8,128)S(1)} %shard_map.72), channel_id=1, replica_groups=mesh['xl'=2,'y'=4,'core'=2,'z'=8,'xh'=2] {'core','z'}, dimensions={0} | all-to-all | bytes 262144 | tf_op jit(solution)/shard_map/all_to_all | solution.py:358
  101.3 5.7 %shard_map.73 = (f32[16,24,128]{2,1,0:T(8,128)S(1)}, bf16[1024,768]{1,0:T(8,128)(2,1)}) custom-call(f32[16,16,128]{2,1,0:T(8,128)S(1)} %all_to_all.38.parts_ref, f32[16,128]{1,0:T(8,128)S(1)} %get-tuple-element.39.logb_ref, f32[1024,1024]{1,0:T(8,128)S(1)} %get-tuple-element.35.ca_ref, f32[1024,1024]{1,0:T(8,128)S(1)} %get-tuple-element.36.cb_ref, ...), custom_call_target="tpu_custom_call" | custom-call | flops 1610612736 | bytes 8388608 | tf_op jit(solution)/shard_map/pallas_call | solution.py:303
  107.0 11.3 %all_to_all.39.parts_ref = f32[16,24,128]{2,1,0:T(8,128)S(1)} all-to-all(f32[16,24,128]{2,1,0:T(8,128)S(1)} %get-tuple-element.41), channel_id=1, replica_groups=mesh['xl'=2,'y'=4,'core'=2,'z'=8,'xh'=2] {'xh','xl','y'}, dimensions={0} | all-to-all | bytes 393216 | tf_op jit(solution)/shard_map/all_to_all | solution.py:369
  118.3 3.7 %all-to-all-start.5 = ((bf16[16,64,768]{2,1,0:T(8,128)(2,1)}), bf16[16,64,768]{2,1,0:T(8,128)(2,1)S(1)}, u32[]{:S(2)}, u32[]{:S(2)}) async-start(bf16[16,64,768]{2,1,0:T(8,128)(2,1)} %bitcast.11), calls=%async_computation.5 | async-start | bytes 3145728 | tf_op jit(solution)/shard_map/all_to_all | solution.py:370
  123.0 3.3 %collective-permute-done.9 = f32[8,128]{1,0:T(8,128)S(1)} collective-permute-done((f32[8,128]{1,0:T(8,128)S(1)}, f32[8,128]{1,0:T(8,128)S(1)}, u32[]{:S(2)}, u32[]{:S(2)}) %collective-permute-start.9) | collective-permute-done | bytes 4128 | tf_op jit(solution)/shard_map/ppermute | solution.py:378
  126.2 0.9 collective-permute-start.10
  127.2 3.6 %collective-permute-done.10 = f32[8,128]{1,0:T(8,128)S(1)} collective-permute-done((f32[8,128]{1,0:T(8,128)S(1)}, f32[8,128]{1,0:T(8,128)S(1)}, u32[]{:S(2)}, u32[]{:S(2)}) %collective-permute-start.10) | collective-permute-done | bytes 4128 | tf_op jit(solution)/shard_map/ppermute | solution.py:378
  130.8 1.5 %collective-permute-start.11 = (f32[8,128]{1,0:T(8,128)S(1)}, f32[8,128]{1,0:T(8,128)S(1)}, u32[]{:S(2)}, u32[]{:S(2)}) collective-permute-start(f32[8,128]{1,0:T(8,128)S(1)} %add.29), channel_id=1, source_target_pairs={{0,8},{2,10},{4,12},{6,14},{8,0},{10,2},{12,4},{14,6},{1,9},{3,11}... | collective-permute-start | bytes 12296 | tf_op jit(solution)/shard_map/ppermute | solution.py:378
  132.3 6.0 %collective-permute-done.11 = f32[8,128]{1,0:T(8,128)S(1)} collective-permute-done((f32[8,128]{1,0:T(8,128)S(1)}, f32[8,128]{1,0:T(8,128)S(1)}, u32[]{:S(2)}, u32[]{:S(2)}) %collective-permute-start.11) | collective-permute-done | bytes 4128 | tf_op jit(solution)/shard_map/ppermute | solution.py:378
  138.9 4.9 %all-to-all-done.5 = bf16[16,64,768]{2,1,0:T(8,128)(2,1)S(1)} async-done(((bf16[16,64,768]{2,1,0:T(8,128)(2,1)}), bf16[16,64,768]{2,1,0:T(8,128)(2,1)S(1)}, u32[]{:S(2)}, u32[]{:S(2)}) %all-to-all-start.5) | async-done | bytes 1572896 | tf_op jit(solution)/shard_map/all_to_all | solution.py:370
  143.8 1.0 multiply_reduce_fusion
  (40 shorter events, 4.8 us)
Async XLA Ops:
  0.6 0.9 copy-start
  1.5 1.3 copy-start.1
  2.9 12.6 %copy-start.4 = (s32[64]{0:T(128)S(1)}, s32[64]{0:T(128)}, u32[]{:S(2)}) copy-start(s32[64]{0:T(128)} %param.7) | copy-start | bytes 772
  2.9 18.8 %copy-start.5 = (s32[128]{0:T(128)S(1)}, s32[128]{0:T(128)}, u32[]{:S(2)}) copy-start(s32[128]{0:T(128)} %param.6) | copy-start | bytes 1540
  2.9 12.5 %collective-permute-start.2 = (bf16[128,768]{1,0:T(8,128)(2,1)S(1)}, bf16[128,768]{1,0:T(8,128)(2,1)S(1)}, u32[]{:S(2)}, u32[]{:S(2)}) collective-permute-start(bf16[128,768]{1,0:T(8,128)(2,1)S(1)} %copy-done.1), channel_id=1, source_target_pairs={{0,12},{2,14},{4,0},{6,2},{8,4},{10,6},{12,8},{14,10},{1,13},{3,15... | collective-permute-start | bytes 589832 | tf_op jit(solution)/shard_map/ppermute | solution.py:314
  8.4 12.7 %collective-permute-start = (bf16[128,768]{1,0:T(8,128)(2,1)S(1)}, bf16[128,768]{1,0:T(8,128)(2,1)S(1)}, u32[]{:S(2)}, u32[]{:S(2)}) collective-permute-start(bf16[128,768]{1,0:T(8,128)(2,1)S(1)} %copy-done.1), channel_id=1, source_target_pairs={{0,4},{2,6},{4,8},{6,10},{8,12},{10,14},{12,0},{14,2},{1,5},{3,7},... | collective-permute-start | bytes 589832 | tf_op jit(solution)/shard_map/ppermute | solution.py:314
  8.4 30.5 %all-to-all-start = ((bf16[16,64,768]{2,1,0:T(8,128)(2,1)}), bf16[16,64,768]{2,1,0:T(8,128)(2,1)S(1)}, u32[]{:S(2)}, u32[]{:S(2)}) async-start(bf16[16,64,768]{2,1,0:T(8,128)(2,1)} %shard_map.67), calls=%async_computation | async-start | bytes 3145728 | tf_op jit(solution)/shard_map/all_to_all | solution.py:324
  15.4 7.4 %collective-permute-start.3 = (bf16[128,768]{1,0:T(8,128)(2,1)S(1)}, bf16[128,768]{1,0:T(8,128)(2,1)S(1)}, u32[]{:S(2)}, u32[]{:S(2)}) collective-permute-start(bf16[128,768]{1,0:T(8,128)(2,1)S(1)} %collective-permute-done.2), channel_id=1, source_target_pairs={{0,14},{2,0},{4,2},{6,4},{8,6},{10,8},{12,10},{14,12},{1,15},{3,1}... | collective-permute-start | bytes 589832 | tf_op jit(solution)/shard_map/ppermute | solution.py:314
  21.0 6.9 %copy-start.2 = (bf16[128,768]{1,0:T(8,128)(2,1)}, bf16[128,768]{1,0:T(8,128)(2,1)S(1)}, u32[]{:S(2)}) copy-start(bf16[128,768]{1,0:T(8,128)(2,1)S(1)} %collective-permute-done) | copy-start | bytes 589828
  21.0 6.0 %collective-permute-start.1 = (bf16[128,768]{1,0:T(8,128)(2,1)S(1)}, bf16[128,768]{1,0:T(8,128)(2,1)S(1)}, u32[]{:S(2)}, u32[]{:S(2)}) collective-permute-start(bf16[128,768]{1,0:T(8,128)(2,1)S(1)} %collective-permute-done), channel_id=1, source_target_pairs={{0,2},{2,4},{4,6},{6,8},{8,10},{10,12},{12,14},{14,0},{1,3},{3,5},... | collective-permute-start | bytes 589832 | tf_op jit(solution)/shard_map/ppermute | solution.py:314
  27.0 6.6 %collective-permute-start.4 = (bf16[128,768]{1,0:T(8,128)(2,1)S(1)}, bf16[128,768]{1,0:T(8,128)(2,1)S(1)}, u32[]{:S(2)}, u32[]{:S(2)}) collective-permute-start(bf16[128,768]{1,0:T(8,128)(2,1)S(1)} %copy-done.1), channel_id=1, source_target_pairs={{0,2},{2,4},{4,6},{6,8},{8,10},{10,12},{12,14},{14,0},{1,3},{3,5},... | collective-permute-start | bytes 589832 | tf_op jit(solution)/shard_map/ppermute | solution.py:314
  28.0 6.2 %collective-permute-start.5 = (bf16[128,768]{1,0:T(8,128)(2,1)S(1)}, bf16[128,768]{1,0:T(8,128)(2,1)S(1)}, u32[]{:S(2)}, u32[]{:S(2)}) collective-permute-start(bf16[128,768]{1,0:T(8,128)(2,1)S(1)} %copy-done.1), channel_id=1, source_target_pairs={{0,14},{2,0},{4,2},{6,4},{8,6},{10,8},{12,10},{14,12},{1,15},{3,1}... | collective-permute-start | bytes 589832 | tf_op jit(solution)/shard_map/ppermute | solution.py:314
  29.8 4.4 %copy-start.3 = (bf16[128,768]{1,0:T(8,128)(2,1)S(1)}, bf16[128,768]{1,0:T(8,128)(2,1)}, u32[]{:S(2)}) copy-start(bf16[128,768]{1,0:T(8,128)(2,1)} %copy-done.2) | copy-start | bytes 589828
  29.8 7.4 %collective-permute-start.7 = (bf16[64,768]{1,0:T(8,128)(2,1)S(1)}, bf16[64,768]{1,0:T(8,128)(2,1)S(1)}, u32[]{:S(2)}, u32[]{:S(2)}) collective-permute-start(bf16[64,768]{1,0:T(8,128)(2,1)S(1)} %slice.10), channel_id=1, source_target_pairs={{0,14},{2,0},{4,2},{6,4},{8,6},{10,8},{12,10},{14,12},{1,15},{3,1}... | collective-permute-start | bytes 294920 | tf_op jit(solution)/shard_map/ppermute | solution.py:314
  32.6 4.6 %collective-permute-start.6 = (bf16[64,768]{1,0:T(8,128)(2,1)S(1)}, bf16[64,768]{1,0:T(8,128)(2,1)S(1)}, u32[]{:S(2)}, u32[]{:S(2)}) collective-permute-start(bf16[64,768]{1,0:T(8,128)(2,1)S(1)} %slice.9), channel_id=1, source_target_pairs={{0,2},{2,4},{4,6},{6,8},{8,10},{10,12},{12,14},{14,0},{1,3},{3,5},... | collective-permute-start | bytes 294920 | tf_op jit(solution)/shard_map/ppermute | solution.py:314
  38.9 3.4 %collective-permute-start.8 = (bf16[1024,768]{1,0:T(8,128)(2,1)S(1)}, bf16[1024,768]{1,0:T(8,128)(2,1)S(1)}, u32[]{:S(2)}, u32[]{:S(2)}) collective-permute-start(bf16[1024,768]{1,0:T(8,128)(2,1)S(1)} %constant_dynamic-update-slice_fusion.y_ref.ya_ref), channel_id=1, source_target_pairs={{0,16},{16,0},{1,17},{17,1},{2,18},{18,2},{3,19},{19,3},{4,20},{20... | collective-permute-start | bytes 4718600 | tf_op jit(solution)/shard_map/ppermute | solution.py:340
  118.3 25.5 %all-to-all-start.5 = ((bf16[16,64,768]{2,1,0:T(8,128)(2,1)}), bf16[16,64,768]{2,1,0:T(8,128)(2,1)S(1)}, u32[]{:S(2)}, u32[]{:S(2)}) async-start(bf16[16,64,768]{2,1,0:T(8,128)(2,1)} %bitcast.11), calls=%async_computation.5 | async-start | bytes 3145728 | tf_op jit(solution)/shard_map/all_to_all | solution.py:370
  122.6 3.6 %collective-permute-start.9 = (f32[8,128]{1,0:T(8,128)S(1)}, f32[8,128]{1,0:T(8,128)S(1)}, u32[]{:S(2)}, u32[]{:S(2)}) collective-permute-start(f32[8,128]{1,0:T(8,128)S(1)} %get-tuple-element.43), channel_id=1, source_target_pairs={{0,2},{2,0},{4,6},{6,4},{8,10},{10,8},{12,14},{14,12},{1,3},{3,1},... | collective-permute-start | bytes 12296 | tf_op jit(solution)/shard_map/ppermute | solution.py:378
  126.2 4.5 %collective-permute-start.10 = (f32[8,128]{1,0:T(8,128)S(1)}, f32[8,128]{1,0:T(8,128)S(1)}, u32[]{:S(2)}, u32[]{:S(2)}) collective-permute-start(f32[8,128]{1,0:T(8,128)S(1)} %add.28), channel_id=1, source_target_pairs={{0,4},{2,6},{4,0},{6,2},{8,12},{10,14},{12,8},{14,10},{1,5},{3,7},... | collective-permute-start | bytes 12296 | tf_op jit(solution)/shard_map/ppermute | solution.py:378
  130.8 7.5 %collective-permute-start.11 = (f32[8,128]{1,0:T(8,128)S(1)}, f32[8,128]{1,0:T(8,128)S(1)}, u32[]{:S(2)}, u32[]{:S(2)}) collective-permute-start(f32[8,128]{1,0:T(8,128)S(1)} %add.29), channel_id=1, source_target_pairs={{0,8},{2,10},{4,12},{6,14},{8,0},{10,2},{12,4},{14,6},{1,9},{3,11}... | collective-permute-start | bytes 12296 | tf_op jit(solution)/shard_map/ppermute | solution.py:378
